TPU v7x, 256 devices: a whole 4x4x8 slice. The times are simulated.
256 devices in a mesh: row: 16 (over z_hi, x), col: 16 (over y, z_lo, core).
Axes of the slice: x: 4, y: 4, z: 8 (z_hi: 4, z_lo: 2; z = z_hi * 2 + z_lo), core: 2. Of those that a mesh axis runs over, the one named last changes fastest.
Arguments:
- object_field: float32 [2, 8192, 8192], P(None, 'row', 'col'), may hold values from -5 to 5
- probe_modes: float32 [4, 2, 128, 128], replicated, may hold values from -5 to 5
- amplitudes: float32 [16, 16, 16, 128, 128], P('row', 'col'), may hold values from 0.5 to 2
- offsets: int32 [16, 16, 16, 2], P('row', 'col'), may hold values from -64 to 447
- counts: int32 [16, 16], P('row', 'col'), may hold values from 1 to 16, as said below
Outputs:
- object_grad: float32 [2, 8192, 8192], P(None, 'row', 'col')
- probe_grad: float32 [4, 2, 128, 128], replicated
Inputs may be any that keep to these rules, and one draw needn't show every extreme that they name: `counts`: live slots come first on each device; some device is full in every draw.
All inputs are finite; a program needn't handle non-finite values.
Results may differ from a plain program's by a relative error of at most 0.0001.
Values sent between devices are 32-bit elements; how exact they have to be, the bound alone decides.
No kernel may reach another device: no remote copies, remote signals or barrier semaphores. Data moves between devices by JAX's collectives and lax.ppermute only.
A program may use at most 64 MiB of HBM per device.

v0:
```python
import math

import jax
import jax.numpy as jnp
from jax import lax
from jax.sharding import PartitionSpec as P


def padded(array, sides, width):
    for axis, dim in sides:
        devices, length = (lax.axis_size(axis), array.shape[dim])
        up = [(i, (i + 1) % devices) for i in range(devices - 1)]
        down = [(j, i) for i, j in up]
        last = lax.slice_in_dim(array, length - width, length, axis=dim)
        initial = lax.slice_in_dim(array, 0, width, axis=dim)
        before = lax.ppermute(last, axis, up)
        after = lax.ppermute(initial, axis, down)
        array = jnp.concatenate([before, array, after], axis=dim)
    return array


def from_behind(value, axis, steps):
    count = lax.axis_size(axis)
    initial, last = (max(0, -steps), min(count, count - steps))
    return lax.ppermute(value, axis, [(source, source + steps) for source in range(initial, last)])


def dft_tables(length):
    indices = jnp.arange(length, dtype=jnp.int32)
    phase_index = indices[:, None] * indices[None, :] % length
    angles = phase_index.astype(jnp.float32) * (2.0 * math.pi / length)
    factor = 1.0 / math.sqrt(length)
    return (jnp.cos(angles) * factor, -jnp.sin(angles) * factor)


def transform(real_part, imag_part, cos_table, sin_table):
    high = lax.Precision.HIGHEST
    left_real = jnp.einsum("jk,mkl->mjl", cos_table, real_part, precision=high) - jnp.einsum(
        "jk,mkl->mjl", sin_table, imag_part, precision=high
    )
    left_imag = jnp.einsum("jk,mkl->mjl", cos_table, imag_part, precision=high) + jnp.einsum(
        "jk,mkl->mjl", sin_table, real_part, precision=high
    )
    out_real = jnp.einsum("mjk,kl->mjl", left_real, cos_table, precision=high) - jnp.einsum(
        "mjk,kl->mjl", left_imag, sin_table, precision=high
    )
    out_imag = jnp.einsum("mjk,kl->mjl", left_real, sin_table, precision=high) + jnp.einsum(
        "mjk,kl->mjl", left_imag, cos_table, precision=high
    )
    return (out_real, out_imag)


def position_terms(patch, amplitude, probe_modes, cos_table, sin_table):
    probe_real = probe_modes[:, 0]
    probe_imag = probe_modes[:, 1]
    object_real = patch[0]
    object_imag = patch[1]
    exit_real = probe_real * object_real - probe_imag * object_imag
    exit_imag = probe_real * object_imag + probe_imag * object_real
    wave_real, wave_imag = transform(exit_real, exit_imag, cos_table, sin_table)
    intensity = jnp.sum(wave_real * wave_real + wave_imag * wave_imag, axis=0)
    residual = 2.0 * (intensity - amplitude * amplitude)
    back_real, back_imag = transform(
        residual[None] * wave_real, residual[None] * wave_imag, cos_table, -sin_table
    )
    grad_real = jnp.sum(probe_real * back_real + probe_imag * back_imag, axis=0)
    grad_imag = jnp.sum(probe_real * back_imag - probe_imag * back_real, axis=0)
    probe_term = jnp.stack(
        [
            object_real * back_real + object_imag * back_imag,
            object_real * back_imag - object_imag * back_real,
        ],
        axis=1,
    )
    return (jnp.stack([grad_real, grad_imag]), probe_term)


def per_device(object_field, probe_modes, amplitudes, offsets, counts):
    patch_size = probe_modes.shape[-1]
    half_width = patch_size // 2
    tile_cells = object_field.shape[1]
    slots = amplitudes.shape[2]
    cos_table, sin_table = dft_tables(patch_size)
    extended = padded(object_field, (("row", 1), ("col", 2)), half_width)
    measured = amplitudes[0, 0]
    starts = offsets[0, 0] + half_width
    live_count = counts[0, 0]

    def extract(slot):
        return lax.dynamic_slice(
            extended, (0, starts[slot, 0], starts[slot, 1]), (2, patch_size, patch_size)
        )

    def deposit(object_total, slot, grad_patch):
        corner = (0, starts[slot, 0], starts[slot, 1])
        current = lax.dynamic_slice(object_total, corner, (2, patch_size, patch_size))
        return lax.dynamic_update_slice(object_total, current + grad_patch, corner)

    def own_step(slot, totals):
        object_total, probe_total = totals
        grad_patch, probe_term = position_terms(
            extract(slot), measured[slot], probe_modes, cos_table, sin_table
        )
        return (deposit(object_total, slot, grad_patch), probe_total + probe_term)

    object_total = jnp.zeros_like(extended)
    probe_total = jnp.zeros_like(probe_modes)
    object_total, probe_total = lax.fori_loop(0, live_count, own_step, (object_total, probe_total))
    received_cols = []
    for shift_by, border in (
        (-1, object_total[:, :, :half_width]),
        (1, object_total[:, :, tile_cells + half_width :]),
    ):
        received_cols.append(from_behind(border, "col", shift_by))
    narrowed = object_total[:, :, half_width : tile_cells + half_width]
    narrowed = (
        narrowed.at[:, :, tile_cells - half_width :]
        .add(received_cols[0])
        .at[:, :, :half_width]
        .add(received_cols[1])
    )
    received_rows = []
    for shift_by, border in (
        (-1, narrowed[:, :half_width, :]),
        (1, narrowed[:, tile_cells + half_width :, :]),
    ):
        received_rows.append(from_behind(border, "row", shift_by))
    object_grad = narrowed[:, half_width : tile_cells + half_width, :]
    object_grad = (
        object_grad.at[:, tile_cells - half_width :, :]
        .add(received_rows[0])
        .at[:, :half_width, :]
        .add(received_rows[1])
    )
    factor = 1.0 / math.sqrt(lax.axis_size("row") * lax.axis_size("col") * slots)
    probe_grad = lax.psum(probe_total, ("row", "col")) * factor
    return (object_grad, probe_grad)


def solution(mesh):
    return jax.shard_map(
        per_device,
        mesh=mesh,
        in_specs=(
            P(None, "row", "col"),
            P(),
            P("row", "col", None, None, None),
            P("row", "col", None, None),
            P("row", "col"),
        ),
        out_specs=(P(None, "row", "col"), P()),
        check_vma=False,
    )
```

profile of v0, /device:TPU:97, one launch (start us, length us, event | category | flops | bytes accessed | tf_op | source)
XLA Modules:
  0.0 770.1 jit_solution(5771009399351935796)
XLA Ops:
  7.2 0.0 all-reduce.2.cloned.1.call-start
  7.2 1.9 copy.41
  9.1 0.0 copy-start.1
  9.2 0.2 fusion.147
  9.4 3.1 collective-permute-start
  12.5 5.2 collective-permute-start.1
  17.7 21.3 %collective-permute-done = f32[2,64,512]{1,2,0:T(8,128)S(1)} collective-permute-done((f32[2,64,512]{1,2,0:T(8,128)S(1)}, f32[2,64,512]{1,2,0:T(8,128)S(1)}, u32[]{:S(2)}, u32[]{:S(2)}) %collective-permute-start) | collective-permute-done | bytes 262176 | tf_op jit(solution)/shard_map/ppermute | solution.py:16
  38.9 0.0 collective-permute-done.1
  38.9 1.1 pad_maximum_fusion.3
  40.0 4.7 collective-permute-start.2
  44.8 1.9 collective-permute-start.3
  46.7 1.1 copy.44
  47.8 3.2 collective-permute-done.2
  51.0 3.4 collective-permute-done.3
  54.4 3.7 pad_maximum_fusion
  58.2 1.9 broadcast_in_dim.4.clone
  60.1 25.4 %while.19 = (s32[]{:T(128)}, f32[2,640,640]{1,2,0:T(8,128)}, f32[4,2,128,128]{3,2,0,1:T(8,128)S(1)}, s32[]{:T(128)}, s32[16,2]{0,1:T(2,128)S(1)}, /*index=5*/f32...) while((s32[]{:T(128)}, f32[2,640,640]{1,2,0:T(8,128)}, ...), condition=%wide.region_4.5_spmd.clone.clone, body=%wide.region_0.4_spmd.clone.clone.sunk | while | flops 1617821696 | bytes 17695016 | solution.py:108
  60.9 0.6 constant_dynamic-slice_fusion.7
  65.4 1.1 constant_dynamic-slice_fusion.9
  66.5 0.1 copy.79
  66.6 0.1 copy.80
  66.7 1.1 constant_dynamic-slice_fusion.8
  67.8 0.1 copy.78
  67.9 0.8 fusion.236
  68.6 0.8 fusion.237
  69.4 0.8 fusion.233
  70.2 0.8 fusion.234
  70.9 0.7 fusion.238
  71.7 0.7 fusion.235
  72.4 0.7 convolution_subtract_fusion.5
  73.1 0.7 add_reduce_fusion.2
  73.9 0.9 fusion.239
  74.7 0.7 fusion.243
  75.5 0.7 fusion.244
  76.2 0.7 fusion.240
  77.0 0.7 fusion.241
  77.7 0.7 fusion.245
  78.5 0.7 fusion.242
  79.2 0.7 convolution_add_fusion.5
  79.9 0.8 add_bitcast_fusion.3
  80.7 0.1 copy.81
  80.8 0.1 maximum_add_fusion.5
  81.0 3.7 dynamic_update_slice.7
  85.5 1.1 fusion.145
  86.7 122.5 %collective-permute-start.4 = (f32[2,640,64]{1,2,0:T(8,128)S(1)}, f32[2,640,64]{1,2,0:T(8,128)S(1)}, u32[]{:S(2)}, u32[]{:S(2)}) collective-permute-start(f32[2,640,64]{1,2,0:T(8,128)S(1)} %get-tuple-element.302), channel_id=1, source_target_pairs={{1,0},{2,1},{3,2},{4,3},{5,4},{6,5},{7,6},{8,7},{9,8},{10,9},{11,1... | collective-permute-start | bytes 983048 | tf_op jit(solution)/shard_map/ppermute | solution.py:25
  209.2 1.9 collective-permute-start.5
  211.1 3.4 slice.148
  214.6 0.8 copy.50
  215.4 0.0 all-reduce.2.cloned.1.call-update
  215.4 0.0 collective-permute-done.4
  215.4 1.7 add_dynamic-update-slice_fusion
  217.2 1.7 fusion.144
  218.9 2.2 fusion.146
  221.1 10.9 %collective-permute-start.6 = (f32[2,64,512]{1,2,0:T(8,128)S(1)}, f32[2,64,512]{1,2,0:T(8,128)S(1)}, u32[]{:S(2)}, u32[]{:S(2)}) collective-permute-start(f32[2,64,512]{1,2,0:T(8,128)S(1)} %get-tuple-element.306), channel_id=1, source_target_pairs={{16,0},{32,16},{48,32},{64,48},{80,64},{96,80},{112,96},{128,112},... | collective-permute-start | bytes 786440 | tf_op jit(solution)/shard_map/ppermute | solution.py:25
  232.1 491.9 %all-reduce.2.cloned.1.call-done = f32[4,2,128,128]{3,2,1,0:T(8,128)} async-done(((f32[4,2,128,128]{3,2,1,0:T(8,128)}), f32[4,2,128,128]{3,2,1,0:T(8,128)}) %all-reduce.2.cloned.1.call-update) | async-done | bytes 524304 | tf_op jit(solution)/shard_map/psum | solution.py:136
  724.0 1.9 broadcast_multiply_fusion
  725.9 2.3 slice.169
  728.2 3.1 collective-permute-start.7
  731.3 1.1 slice_add_fusion.1
  732.4 2.9 scatter-add.16
  735.3 21.1 %collective-permute-done.7 = f32[2,64,512]{1,2,0:T(8,128)} collective-permute-done((f32[2,64,512]{1,2,0:T(8,128)}, f32[2,64,512]{1,2,0:T(8,128)}, u32[]{:S(2)}, u32[]{:S(2)}) %collective-permute-start.7) | collective-permute-done | bytes 262176 | tf_op jit(solution)/shard_map/ppermute | solution.py:25
  756.4 1.1 slice_add_fusion
  757.6 3.8 scatter-add.19
  761.4 1.8 copy.51
  (8 shorter events, 0.1 us)
Async XLA Ops:
  7.2 716.8 %all-reduce.2.cloned.1.call-start = ((), (), s32[]{:S(2)}) async-start(), calls=%async_computation | async-start | bytes 1048576 | tf_op jit(solution)/shard_map/psum | solution.py:136
  9.1 38.7 %copy-start.1 = (s32[1,1,16,2]{2,3,1,0:T(2,128)S(1)}, s32[1,1,16,2]{2,3,1,0:T(2,128)}, u32[]{:S(2)}) copy-start(s32[1,1,16,2]{2,3,1,0:T(2,128)} %param.18) | copy-start | bytes 388
  9.4 29.6 %collective-permute-start = (f32[2,64,512]{1,2,0:T(8,128)S(1)}, f32[2,64,512]{1,2,0:T(8,128)S(1)}, u32[]{:S(2)}, u32[]{:S(2)}) collective-permute-start(f32[2,64,512]{1,2,0:T(8,128)S(1)} %get-tuple-element.307), channel_id=1, source_target_pairs={{0,16},{16,32},{32,48},{48,64},{64,80},{80,96},{96,112},{112,128},... | collective-permute-start | bytes 786440 | tf_op jit(solution)/shard_map/ppermute | solution.py:16
  12.5 26.4 %collective-permute-start.1 = (f32[2,64,512]{1,2,0:T(8,128)S(1)}, f32[2,64,512]{1,2,0:T(8,128)S(1)}, u32[]{:S(2)}, u32[]{:S(2)}) collective-permute-start(f32[2,64,512]{1,2,0:T(8,128)S(1)} %get-tuple-element.308), channel_id=1, source_target_pairs={{16,0},{32,16},{48,32},{64,48},{80,64},{96,80},{112,96},{128,112},... | collective-permute-start | bytes 786440 | tf_op jit(solution)/shard_map/ppermute | solution.py:17
  38.9 7.8 %copy-start = (f32[2,64,512]{1,2,0:T(8,128)}, f32[2,64,512]{1,2,0:T(8,128)S(1)}, u32[]{:S(2)}) copy-start(f32[2,64,512]{1,2,0:T(8,128)S(1)} %collective-permute-done.1) | copy-start | bytes 786436
  40.0 11.0 %collective-permute-start.2 = (f32[2,640,64]{1,2,0:T(8,128)}, f32[2,640,64]{1,2,0:T(8,128)S(1)}, u32[]{:S(2)}, u32[]{:S(2)}) collective-permute-start(f32[2,640,64]{1,2,0:T(8,128)} %get-tuple-element.303), channel_id=1, source_target_pairs={{0,1},{1,2},{2,3},{3,4},{4,5},{5,6},{6,7},{7,8},{8,9},{9,10},{10,1... | collective-permute-start | bytes 983048 | tf_op jit(solution)/shard_map/ppermute | solution.py:16
  44.8 9.6 %collective-permute-start.3 = (f32[2,640,64]{1,2,0:T(8,128)}, f32[2,640,64]{1,2,0:T(8,128)}, u32[]{:S(2)}, u32[]{:S(2)}) collective-permute-start(f32[2,640,64]{1,2,0:T(8,128)} %get-tuple-element.304), channel_id=1, source_target_pairs={{1,0},{2,1},{3,2},{4,3},{5,4},{6,5},{7,6},{8,7},{9,8},{10,9},{11,1... | collective-permute-start | bytes 983048 | tf_op jit(solution)/shard_map/ppermute | solution.py:17
  86.7 128.8 %collective-permute-start.4 = (f32[2,640,64]{1,2,0:T(8,128)S(1)}, f32[2,640,64]{1,2,0:T(8,128)S(1)}, u32[]{:S(2)}, u32[]{:S(2)}) collective-permute-start(f32[2,640,64]{1,2,0:T(8,128)S(1)} %get-tuple-element.302), channel_id=1, source_target_pairs={{1,0},{2,1},{3,2},{4,3},{5,4},{6,5},{7,6},{8,7},{9,8},{10,9},{11,1... | collective-permute-start | bytes 983048 | tf_op jit(solution)/shard_map/ppermute | solution.py:25
  209.2 8.0 %collective-permute-start.5 = (f32[2,640,64]{1,2,0:T(8,128)S(1)}, f32[2,640,64]{1,2,0:T(8,128)S(1)}, u32[]{:S(2)}, u32[]{:S(2)}) collective-permute-start(f32[2,640,64]{1,2,0:T(8,128)S(1)} %get-tuple-element.301), channel_id=1, source_target_pairs={{0,1},{1,2},{2,3},{3,4},{4,5},{5,6},{6,7},{7,8},{8,9},{9,10},{10,1... | collective-permute-start | bytes 983048 | tf_op jit(solution)/shard_map/ppermute | solution.py:25
  221.1 510.2 %collective-permute-start.6 = (f32[2,64,512]{1,2,0:T(8,128)S(1)}, f32[2,64,512]{1,2,0:T(8,128)S(1)}, u32[]{:S(2)}, u32[]{:S(2)}) collective-permute-start(f32[2,64,512]{1,2,0:T(8,128)S(1)} %get-tuple-element.306), channel_id=1, source_target_pairs={{16,0},{32,16},{48,32},{64,48},{80,64},{96,80},{112,96},{128,112},... | collective-permute-start | bytes 786440 | tf_op jit(solution)/shard_map/ppermute | solution.py:25
  728.2 28.2 %collective-permute-start.7 = (f32[2,64,512]{1,2,0:T(8,128)}, f32[2,64,512]{1,2,0:T(8,128)}, u32[]{:S(2)}, u32[]{:S(2)}) collective-permute-start(f32[2,64,512]{1,2,0:T(8,128)} %get-tuple-element.305), channel_id=1, source_target_pairs={{0,16},{16,32},{32,48},{48,64},{64,80},{80,96},{96,112},{112,128},... | collective-permute-start | bytes 786440 | tf_op jit(solution)/shard_map/ppermute | solution.py:25
Sparse Core Ops, SparseCore 0:
  215.6 508.3 all-reduce.1
where the time goes:
time: 775 us; the launch traced here: 770 us
  waiting for transfers between devices  541 us (70%)
  starting transfers between devices  153 us (20%)
  local copies, waits for them, and re-layouts  30.5 us (4%)
  between operations  14.2 us (2%)
  other arithmetic  13.4 us (2%)
  matrix products  11.9 us (2%)
    psum x1, waiting for transfers between devices, per_device(): probe_grad = lax.psum(probe_total, ('row', 'col')) * factor  492 us
    ppermute x4, starting transfers between devices, from_behind(): lax.ppermute(value, axis, [(source, source + steps) for source in range(i...  138 us
    ppermute x2, waiting for transfers between devices, padded(): before = lax.ppermute(last, axis, up)  24.4 us
    ppermute x4, waiting for transfers between devices, from_behind(): lax.ppermute(value, axis, [(source, source + steps) for source in range(i...  21.1 us
  transfers between devices with their start and end apart: 9, of which 5 were waited for; matrix products, arithmetic and copies ran while one was open for 2% of the time, Pallas kernels for 0%

commit v1 on v0

v1 whole, which is shorter than its diff:
```python
import functools
import math

import jax
import jax.numpy as jnp
import ml_dtypes
import numpy as np
from jax import lax
from jax.experimental import pallas as pl
from jax.experimental.pallas import tpu as pltpu
from jax.sharding import Mesh
from jax.sharding import PartitionSpec as P

PATCH = 128
MODES = 4
TILE = 512
SLOTS = 16
HALF = 64
EXT = TILE + 2 * HALF
BLOCKS = 6
UNROLL = 2

ROW = ("zh", "x")
COL = ("y", "zl", "core")


def split_table(table):
    high = table.astype(np.float32).astype(ml_dtypes.bfloat16)
    low = (table - high.astype(np.float64)).astype(np.float32).astype(ml_dtypes.bfloat16)
    return high, low


def dft_tables(n):
    i = np.arange(n)
    angles = (np.outer(i, i) % n) * (2 * math.pi / n)
    cos, sin = np.cos(angles) / math.sqrt(n), -np.sin(angles) / math.sqrt(n)
    forward = np.block([[cos, sin], [-sin, cos]])
    fh, fl = split_table(forward)
    ih, il = split_table(forward.T)
    return (
        np.concatenate([fh, fh, fl], 0),
        np.concatenate([ih, il, ih], 1),
        np.concatenate([fh, fl, fh], 1),
        np.concatenate([ih, ih, il], 0),
    )


def split(x):
    high = x.astype(jnp.bfloat16)
    return high, (x - high.astype(jnp.float32)).astype(jnp.bfloat16)


def dot(a, b):
    return jnp.dot(a, b, preferred_element_type=jnp.float32)


def right_dft(x, table):
    high, low = split(x)
    return dot(jnp.concatenate([high, low, high], 1), table)


def left_dft(table, x):
    high, low = split(x)
    return dot(table, jnp.concatenate([high, high, low], 0))


def to_cols(y):
    n = PATCH
    return jnp.concatenate(
        [jnp.concatenate([y[m * n : (m + 1) * n, p * n : (p + 1) * n] for m in range(MODES)], 1) for p in range(2)], 0
    )


def to_rows(z):
    n = PATCH
    return jnp.concatenate(
        [jnp.concatenate([z[p * n : (p + 1) * n, m * n : (m + 1) * n] for p in range(2)], 1) for m in range(MODES)], 0
    )


def lane_iota(rows):
    return lax.broadcasted_iota(jnp.int32, (rows, PATCH), 1)


def is_inside(offsets, k):
    r, c = offsets[2 * k], offsets[2 * k + 1]
    top = TILE - PATCH
    return (r >= 0) & (r <= top) & (c >= 0) & (c <= top)


def early_slots(counts, offsets):
    live = counts[0]

    def tally(k, total):
        return total + jnp.where(is_inside(offsets, k) & (k < live), 1, 0)

    inside = lax.fori_loop(0, SLOTS, tally, 0)
    return live, inside // UNROLL * UNROLL


def choose_slots(counts, offsets, chosen, early):
    live, first = early_slots(counts, offsets)

    def pick(k, state):
        seen, size = state
        inner = is_inside(offsets, k)
        is_early = inner & (seen < first)
        chosen[size] = k
        take = (is_early == early) & (k < live)
        seen = seen + jnp.where(inner, 1, 0)
        return seen, size + jnp.where(take, 1, 0)

    _, size = lax.fori_loop(0, SLOTS, pick, (0, 0))
    return size


def slot_work(k, out_slot, scale, offsets, extended, amplitudes, probe, tables, patch_grads, probe_total):
    rf, lf, li, ri = tables
    n = PATCH
    row = offsets[2 * k] + HALF
    col = offsets[2 * k + 1] + PATCH
    block = col // n
    lead = col - block * n
    turn = jnp.where(lead == 0, 0, n - lead)
    lane = lane_iota(n)
    parts = []
    for p in range(2):
        a = pltpu.roll(extended[p, block, pl.ds(row, n), :], turn, 1)
        b = pltpu.roll(extended[p, block + 1, pl.ds(row, n), :], turn, 1)
        parts.append(jnp.where(lane < n - lead, a, b))
    obj_r, obj_i = parts
    waves = []
    for m in range(MODES):
        pr, pi = probe[m, 0], probe[m, 1]
        waves.append(jnp.concatenate([pr * obj_r - pi * obj_i, pr * obj_i + pi * obj_r], 1))
    far = left_dft(lf[...], to_cols(right_dft(jnp.concatenate(waves, 0), rf[...])))
    power = far * far
    power = power[:n] + power[n:]
    intensity = power[:, :n] + power[:, n : 2 * n] + power[:, 2 * n : 3 * n] + power[:, 3 * n :]
    measured = amplitudes[k]
    residual = (intensity - measured * measured) * scale
    weighted = far * jnp.concatenate([jnp.concatenate([residual] * MODES, 1)] * 2, 0)
    back = right_dft(to_rows(left_dft(li[...], weighted)), ri[...])
    total_r = total_i = None
    for m in range(MODES):
        gr, gi = back[m * n : (m + 1) * n, :n], back[m * n : (m + 1) * n, n:]
        pr, pi = probe[m, 0], probe[m, 1]
        tr, ti = pr * gr + pi * gi, pr * gi - pi * gr
        total_r, total_i = (tr, ti) if m == 0 else (total_r + tr, total_i + ti)
        probe_total[m, 0] += obj_r * gr + obj_i * gi
        probe_total[m, 1] += obj_r * gi - obj_i * gr
    patch_grads[out_slot, 0] = total_r
    patch_grads[out_slot, 1] = total_i


def run_slots(counts, offsets, chosen, early, *work):
    size = choose_slots(counts, offsets, chosen, early)

    def step(j, carry):
        for u in range(UNROLL):
            i = j * UNROLL + u
            on = i < size
            k = jnp.where(on, chosen[jnp.minimum(i, SLOTS - 1)], 0)
            slot_work(k, jnp.where(on, k, SLOTS), jnp.where(on, 2.0, 0.0), offsets, *work)
        return carry

    lax.fori_loop(0, (size + UNROLL - 1) // UNROLL, step, 0)


def tile_copies(tile, extended, sem):
    return [
        pltpu.make_async_copy(
            tile.at[:, :, pl.ds(b * PATCH, PATCH)], extended.at[:, b + 1, pl.ds(HALF, TILE), :], sem
        )
        for b in range(TILE // PATCH)
    ]


def early_kernel(counts, offsets, tile, amps, probe, rf, lf, li, ri, patch_grads, probe_total, extended, chosen, sem):
    copies = tile_copies(tile, extended, sem)
    for c in copies:
        c.start()
    probe_total[...] = jnp.zeros_like(probe_total)
    for c in copies:
        c.wait()
    run_slots(counts, offsets, chosen, True, extended, amps, probe, (rf, lf, li, ri), patch_grads, probe_total)


def late_kernel(
    counts, offsets, tile, above, below, left, right, amps, probe, rf, lf, li, ri, probe_before,
    patch_grads, probe_total, extended, chosen, sem
):
    copies = tile_copies(tile, extended, sem)
    for b in range(TILE // PATCH):
        lanes = pl.ds(b * PATCH, PATCH)
        copies.append(pltpu.make_async_copy(above.at[:, :, lanes], extended.at[:, b + 1, pl.ds(0, HALF), :], sem))
        copies.append(
            pltpu.make_async_copy(below.at[:, :, lanes], extended.at[:, b + 1, pl.ds(HALF + TILE, HALF), :], sem)
        )
    for c in copies:
        c.start()
    probe_total[...] = probe_before[...]
    extended[0, 0] = pltpu.roll(left[...], HALF, 1)
    extended[1, 0] = left[...]
    extended[0, BLOCKS - 1] = right[...]
    extended[1, BLOCKS - 1] = pltpu.roll(right[...], HALF, 1)
    for c in copies:
        c.wait()
    run_slots(counts, offsets, chosen, False, extended, amps, probe, (rf, lf, li, ri), patch_grads, probe_total)


def pack_kernel(above, below, first, last, left_send, right_send):
    def pack(rows, a, b):
        low = lane_iota(rows) < HALF
        left_send_part = jnp.where(low, a[0], pltpu.roll(a[1], HALF, 1))
        right_send_part = jnp.where(low, pltpu.roll(b[0], HALF, 1), b[1])
        return left_send_part, right_send_part

    end = TILE - PATCH
    for start, rows, a, b in (
        (0, HALF, above[:, :, :PATCH], above[:, :, end:]),
        (HALF, TILE, first[...], last[...]),
        (HALF + TILE, HALF, below[:, :, :PATCH], below[:, :, end:]),
    ):
        left_send[start : start + rows, :], right_send[start : start + rows, :] = pack(rows, a, b)


def deposit_kernel(counts, offsets, early_grads, late_grads, middle, left_send, right_send, total, held, sems):
    n = PATCH
    live, first = early_slots(counts, offsets)

    def fetch(k, seen, buffer):
        is_early = is_inside(offsets, k) & (seen < first)

        @pl.when(is_early)
        def _():
            pltpu.make_async_copy(early_grads.at[k], held.at[k], sems.at[k]).start()

        @pl.when(jnp.logical_not(is_early))
        def _():
            pltpu.make_async_copy(late_grads.at[k], held.at[k], sems.at[k]).start()

        return seen + jnp.where(is_inside(offsets, k), 1, 0)

    lax.fori_loop(0, live, lambda k, seen: fetch(k, seen, 0), 0)
    total[...] = jnp.zeros_like(total)
    lane = lane_iota(n)

    def add(k, carry):
        pltpu.make_async_copy(early_grads.at[k], held.at[k], sems.at[k]).wait()
        row = offsets[2 * k] + HALF
        col = offsets[2 * k + 1] + n
        block = col // n
        lead = col - block * n
        for p in range(2):
            turned = pltpu.roll(held[k, p], lead, 1)
            total[p, block, pl.ds(row, n), :] += jnp.where(lane >= lead, turned, 0.0)
            total[p, block + 1, pl.ds(row, n), :] += jnp.where(lane < lead, turned, 0.0)
        return carry

    lax.fori_loop(0, live, add, 0)
    for b in range(TILE // n):
        middle[:, :, b * n : (b + 1) * n] = total[:, b + 1]
    low = lane_iota(EXT) < HALF
    left_send[...] = jnp.where(low, pltpu.roll(total[0, 0], HALF, 1), total[1, 0])
    right_send[...] = jnp.where(low, total[0, BLOCKS - 1], pltpu.roll(total[1, BLOCKS - 1], HALF, 1))


def add_sides(rows, middle, from_left, from_right):
    low = lane_iota(rows) < HALF
    first = [
        middle[0, :, :PATCH] + jnp.where(low, from_left, 0.0),
        middle[1, :, :PATCH] + jnp.where(low, pltpu.roll(from_left, HALF, 1), 0.0),
    ]
    end = TILE - PATCH
    last = [
        middle[0, :, end:] + jnp.where(low, 0.0, pltpu.roll(from_right, HALF, 1)),
        middle[1, :, end:] + jnp.where(low, 0.0, from_right),
    ]
    return [jnp.concatenate([first[p], middle[p, :, PATCH:end], last[p]], 1) for p in range(2)]


def edges_kernel(middle_top, middle_bottom, from_left, from_right, top_send, bottom_send):
    for part, rows, out in (
        (middle_top, slice(0, HALF), top_send),
        (middle_bottom, slice(HALF + TILE, EXT), bottom_send),
    ):
        out[0], out[1] = add_sides(HALF, part[...], from_left[rows, :], from_right[rows, :])


def merge_kernel(middle, from_left, from_right, from_above, from_below, out):
    rows = slice(HALF, HALF + TILE)
    whole = add_sides(TILE, middle[:, rows, :], from_left[rows, :], from_right[rows, :])
    for p in range(2):
        out[p, HALF : TILE - HALF, :] = whole[p][HALF : TILE - HALF]
        out[p, :HALF, :] = whole[p][:HALF] + from_above[p]
        out[p, TILE - HALF :, :] = whole[p][TILE - HALF :] + from_below[p]


VMEM = pl.BlockSpec(memory_space=pltpu.VMEM)
SMEM = pl.BlockSpec(memory_space=pltpu.SMEM)
ANY = pl.BlockSpec(memory_space=pl.ANY)


def call(kernel, in_specs, out_shapes, scratch, *args, out_specs=None):
    return pl.pallas_call(
        kernel,
        in_specs=in_specs,
        out_specs=out_specs or [VMEM] * len(out_shapes),
        out_shape=[jax.ShapeDtypeStruct(s, jnp.float32) for s in out_shapes],
        scratch_shapes=scratch,
        compiler_params=pltpu.CompilerParams(vmem_limit_bytes=48 * 2**20),
    )(*args)


def shift(value, axes, count, step):
    pairs = [(i, i + step) for i in range(count) if 0 <= i + step < count]
    return lax.ppermute(value, axes, pairs)


def swap(value, axis, bit, size):
    return lax.ppermute(value, axis, [(i, i ^ (1 << bit)) for i in range(size)])


def all_sum(x, sizes):
    halved = [("core", 0), ("zl", 0), ("y", 0), ("y", 1)]
    doubled = [("x", 0), ("x", 1), ("zh", 0), ("zh", 1)]
    for axis, bit in halved:
        half = x.shape[0] // 2
        mine = (lax.axis_index(axis) >> bit) & 1
        kept = lax.dynamic_slice_in_dim(x, mine * half, half, 0)
        sent = lax.dynamic_slice_in_dim(x, (1 - mine) * half, half, 0)
        x = kept + swap(sent, axis, bit, sizes[axis])
    for axis, bit in doubled:
        x = x + swap(x, axis, bit, sizes[axis])
    for axis, bit in reversed(halved):
        mine = (lax.axis_index(axis) >> bit) & 1
        other = swap(x, axis, bit, sizes[axis])
        x = jnp.where(mine == 0, jnp.concatenate([x, other], 0), jnp.concatenate([other, x], 0))
    return x


def per_device(sizes, tile, probe, amplitudes, offsets, counts):
    rows, cols = sizes["zh"] * sizes["x"], sizes["y"] * sizes["zl"] * sizes["core"]
    tables = [jnp.asarray(t) for t in dft_tables(PATCH)]
    counts = counts.reshape(1)
    offsets = offsets.reshape(2 * SLOTS)
    amps = amplitudes.reshape(SLOTS, PATCH, PATCH)
    from_above = shift(tile[:, TILE - HALF :, :], ROW, rows, 1)
    from_below = shift(tile[:, :HALF, :], ROW, rows, -1)
    slot_scratch = [
        pltpu.VMEM((2, BLOCKS, EXT, PATCH), jnp.float32),
        pltpu.SMEM((SLOTS + 1,), jnp.int32),
        pltpu.SemaphoreType.DMA,
    ]
    slot_shapes = [(SLOTS + 1, 2, PATCH, PATCH), (MODES, 2, PATCH, PATCH)]
    early_grads, probe_early = call(
        early_kernel, [SMEM, SMEM, ANY] + [VMEM] * 6, slot_shapes, slot_scratch, counts, offsets, tile, amps, probe, *tables
    )
    left_send, right_send = call(
        pack_kernel, [VMEM] * 4, [(EXT, PATCH)] * 2, [], from_above, from_below, tile[:, :, :PATCH], tile[:, :, TILE - PATCH :]
    )
    from_left = shift(right_send, COL, cols, 1)
    from_right = shift(left_send, COL, cols, -1)
    late_grads, probe_total = call(
        late_kernel, [SMEM, SMEM] + [ANY] * 3 + [VMEM] * 9, slot_shapes, slot_scratch,
        counts, offsets, tile, from_above, from_below, from_left, from_right, amps, probe, *tables, probe_early
    )
    factor = 1.0 / math.sqrt(rows * cols * SLOTS)
    summed = all_sum(probe_total.reshape(-1, PATCH), sizes)
    probe_grad = (summed * factor).reshape(MODES, 2, PATCH, PATCH)
    middle, left_out, right_out = call(
        deposit_kernel, [SMEM, SMEM, ANY, ANY], [(2, EXT, TILE), (EXT, PATCH), (EXT, PATCH)],
        [
            pltpu.VMEM((2, BLOCKS, EXT, PATCH), jnp.float32),
            pltpu.VMEM((SLOTS, 2, PATCH, PATCH), jnp.float32),
            pltpu.SemaphoreType.DMA((SLOTS,)),
        ],
        counts, offsets, early_grads, late_grads
    )
    grad_left = shift(right_out, COL, cols, 1)
    grad_right = shift(left_out, COL, cols, -1)
    top_out, bottom_out = call(
        edges_kernel, [VMEM] * 4, [(2, HALF, TILE)] * 2, [],
        middle[:, :HALF, :], middle[:, HALF + TILE :, :], grad_left, grad_right
    )
    grad_above = shift(bottom_out, ROW, rows, 1)
    grad_below = shift(top_out, ROW, rows, -1)
    (object_grad,) = call(
        merge_kernel, [VMEM] * 5, [(2, TILE, TILE)], [], middle, grad_left, grad_right, grad_above, grad_below
    )
    return object_grad, probe_grad


def solution(mesh):
    sizes = {"zh": 4, "x": 4, "y": 4, "zl": 2, "core": 2}
    fine = Mesh(mesh.devices.reshape(tuple(sizes.values())), tuple(sizes))
    return jax.shard_map(
        functools.partial(per_device, sizes),
        mesh=fine,
        in_specs=(P(None, ROW, COL), P(), P(ROW, COL), P(ROW, COL), P(ROW, COL)),
        out_specs=(P(None, ROW, COL), P()),
        check_vma=False,
    )
```

time: 775 us -> 168 us (0.22)
  the two profiles are of different devices: /device:TPU:97 before, /device:TPU:15 now
where the time goes in v1:
time: 168 us; the launch traced here: 169 us
  starting transfers between devices  64.7 us (39%)
  waiting for transfers between devices  58.8 us (35%)
  Pallas kernels  29 us (17%)
  local copies, waits for them, and re-layouts  10.6 us (6%)
  other arithmetic  3.81 us (2%)
  between operations  1.69 us (1%)
    ppermute x8, starting transfers between devices, shift(): return lax.ppermute(value, axes, pairs)  36.8 us
    ppermute x12, waiting for transfers between devices, swap(): return lax.ppermute(value, axis, [(i, i ^ 1 << bit) for i in range(size)])  30.3 us
    pallas_call x6, Pallas kernels, call(): pl.pallas_call(kernel, in_specs=in_specs, out_specs=out_specs or [VMEM] *...  29 us
    ppermute x8, waiting for transfers between devices, shift(): return lax.ppermute(value, axes, pairs)  28.5 us
    ppermute x12, starting transfers between devices, swap(): return lax.ppermute(value, axis, [(i, i ^ 1 << bit) for i in range(size)])  27.9 us
    unnamed x31, local copies, waits for them, and re-layouts  5.78 us
  transfers between devices with their start and end apart: 20, of which 13 were waited for; matrix products, arithmetic and copies ran while one was open for 2% of the time, Pallas kernels for 10%

profile of v1, /device:TPU:15, one launch (start us, length us, event | category | flops | bytes accessed | tf_op | source)
XLA Modules:
  0.0 168.6 jit_solution(16026312820605632659)
XLA Ops:
  0.6 0.0 copy-start.6
  0.6 0.0 copy-start
  0.7 1.2 fusion.3
  1.9 4.8 %collective-permute-start = (f32[2,64,512]{2,1,0:T(8,128)S(1)}, f32[2,64,512]{2,1,0:T(8,128)S(1)}, u32[]{:S(2)}, u32[]{:S(2)}) collective-permute-start(f32[2,64,512]{2,1,0:T(8,128)S(1)} %get-tuple-element.29), channel_id=1, source_target_pairs={{0,16},{16,32},{32,48},{48,64},{64,80},{80,96},{96,112},{112,128},... | collective-permute-start | bytes 786440 | tf_op jit(solution)/shard_map/ppermute | solution.py:318
  6.7 1.9 %collective-permute-start.1 = (f32[2,64,512]{2,1,0:T(8,128)S(1)}, f32[2,64,512]{2,1,0:T(8,128)S(1)}, u32[]{:S(2)}, u32[]{:S(2)}) collective-permute-start(f32[2,64,512]{2,1,0:T(8,128)S(1)} %get-tuple-element.28), channel_id=1, source_target_pairs={{16,0},{32,16},{48,32},{64,48},{80,64},{96,80},{112,96},{128,112},... | collective-permute-start | bytes 786440 | tf_op jit(solution)/shard_map/ppermute | solution.py:318
  8.6 1.3 fusion.2
  9.9 1.8 %collective-permute-done.above = f32[2,64,512]{2,1,0:T(8,128)S(1)} collective-permute-done((f32[2,64,512]{2,1,0:T(8,128)S(1)}, f32[2,64,512]{2,1,0:T(8,128)S(1)}, u32[]{:S(2)}, u32[]{:S(2)}) %collective-permute-start) | collective-permute-done | bytes 262176 | tf_op jit(solution)/shard_map/ppermute | solution.py:318
  11.7 12.4 %collective-permute-done.1.below = f32[2,64,512]{2,1,0:T(8,128)S(1)} collective-permute-done((f32[2,64,512]{2,1,0:T(8,128)S(1)}, f32[2,64,512]{2,1,0:T(8,128)S(1)}, u32[]{:S(2)}, u32[]{:S(2)}) %collective-permute-start.1) | collective-permute-done | bytes 262176 | tf_op jit(solution)/shard_map/ppermute | solution.py:318
  24.1 1.1 shard_map.105
  25.2 1.9 %collective-permute-start.2 = (f32[640,128]{1,0:T(8,128)}, f32[640,128]{1,0:T(8,128)}, u32[]{:S(2)}, u32[]{:S(2)}) collective-permute-start(f32[640,128]{1,0:T(8,128)} %get-tuple-element.14), channel_id=1, source_target_pairs={{0,1},{1,2},{2,3},{3,4},{4,5},{5,6},{6,7},{7,8},{8,9},{9,10},{10,1... | collective-permute-start | bytes 983048 | tf_op jit(solution)/shard_map/ppermute | solution.py:318
  27.1 3.8 %collective-permute-start.3 = (f32[640,128]{1,0:T(8,128)}, f32[640,128]{1,0:T(8,128)}, u32[]{:S(2)}, u32[]{:S(2)}) collective-permute-start(f32[640,128]{1,0:T(8,128)} %get-tuple-element.15), channel_id=1, source_target_pairs={{1,0},{2,1},{3,2},{4,3},{5,4},{6,5},{7,6},{8,7},{9,8},{10,9},{11,1... | collective-permute-start | bytes 983048 | tf_op jit(solution)/shard_map/ppermute | solution.py:318
  31.0 0.1 copy.12
  31.1 0.1 reshape.24.offsets
  31.8 0.0 copy-done.6
  31.9 0.0 copy-start.5
  31.9 1.0 copy-done.5
  32.9 1.0 copy-done.7
  33.9 1.0 copy-done.8
  34.9 1.0 copy-done.9
  35.9 8.9 %shard_map.104 = (f32[17,2,128,128]{3,2,1,0:T(8,128)}, f32[4,2,128,128]{3,2,1,0:T(8,128)S(1)}) custom-call(s32[1]{0:T(128)} %bitcast.6.counts, s32[32]{0:T(128)S(1)} %reshape.24.offsets, f32[2,512,512]{2,1,0:T(8,128)S(1)} %copy-done, f32[16,128,128]{2,1,0:T(8,128)S(1)} %bitcast.9, f32[4,2,128,128]{3,2,1,0:T(8,128)S(1)} %copy-done.5, ...), custom_call_target="tpu_custom_call" | custom-call | tf_op jit(solution)/shard_map/pallas_call | solution.py:306
  44.8 0.0 collective-permute-done.2.left
  44.8 0.0 collective-permute-done.3.right
  44.8 10.4 %shard_map.106 = (f32[17,2,128,128]{3,2,1,0:T(8,128)}, f32[4,2,128,128]{3,2,1,0:T(8,128)}) custom-call(s32[1]{0:T(128)} %bitcast.7.counts, s32[32]{0:T(128)S(1)} %reshape.24.offsets, f32[2,512,512]{2,1,0:T(8,128)} %tile.3, f32[2,64,512]{2,1,0:T(8,128)S(1)} %copy-done.11, f32[2,64,512]{2,1,0:T(8,128)S(1)} %copy-done.13, ...), custom_call_target="tpu_custom_call" | custom-call | tf_op jit(solution)/shard_map/pallas_call | solution.py:306
  55.2 1.1 constant_dynamic-slice_fusion.3
  56.3 15.1 %collective-permute-start.8 = (f32[512,128]{1,0:T(8,128)S(1)}, f32[512,128]{1,0:T(8,128)S(1)}, u32[]{:S(2)}, u32[]{:S(2)}) collective-permute-start(f32[512,128]{1,0:T(8,128)S(1)} %constant_dynamic-slice_fusion.3), channel_id=1, source_target_pairs={{0,1},{1,0},{2,3},{3,2},{4,5},{5,4},{6,7},{7,6},{8,9},{9,8},{10,11... | collective-permute-start | bytes 786440 | tf_op jit(solution)/shard_map/ppermute | solution.py:322
  71.5 1.2 collective-permute-done.8
  72.6 1.0 dynamic-slice_add_fusion
  73.6 0.1 collective-permute-start.9
  73.7 4.7 %collective-permute-done.9 = f32[256,128]{1,0:T(8,128)S(1)} collective-permute-done((f32[256,128]{1,0:T(8,128)S(1)}, f32[256,128]{1,0:T(8,128)S(1)}, u32[]{:S(2)}, u32[]{:S(2)}) %collective-permute-start.9) | collective-permute-done | bytes 131104 | tf_op jit(solution)/shard_map/ppermute | solution.py:322
  78.5 0.1 collective-permute-start.10
  78.6 3.1 %collective-permute-done.10 = f32[128,128]{1,0:T(8,128)S(1)} collective-permute-done((f32[128,128]{1,0:T(8,128)S(1)}, f32[128,128]{1,0:T(8,128)S(1)}, u32[]{:S(2)}, u32[]{:S(2)}) %collective-permute-start.10) | collective-permute-done | bytes 65568 | tf_op jit(solution)/shard_map/ppermute | solution.py:322
  81.7 0.1 collective-permute-start.11
  81.8 4.3 %collective-permute-done.11 = f32[64,128]{1,0:T(8,128)S(1)} collective-permute-done((f32[64,128]{1,0:T(8,128)S(1)}, f32[64,128]{1,0:T(8,128)S(1)}, u32[]{:S(2)}, u32[]{:S(2)}) %collective-permute-start.11) | collective-permute-done | bytes 32800 | tf_op jit(solution)/shard_map/ppermute | solution.py:322
  86.1 0.0 collective-permute-start.12
  86.1 3.1 %collective-permute-done.12 = f32[64,128]{1,0:T(8,128)S(1)} collective-permute-done((f32[64,128]{1,0:T(8,128)S(1)}, f32[64,128]{1,0:T(8,128)S(1)}, u32[]{:S(2)}, u32[]{:S(2)}) %collective-permute-start.12) | collective-permute-done | bytes 32800 | tf_op jit(solution)/shard_map/ppermute | solution.py:322
  89.1 0.0 collective-permute-start.13
  89.1 4.3 %collective-permute-done.13 = f32[64,128]{1,0:T(8,128)S(1)} collective-permute-done((f32[64,128]{1,0:T(8,128)S(1)}, f32[64,128]{1,0:T(8,128)S(1)}, u32[]{:S(2)}, u32[]{:S(2)}) %collective-permute-start.13) | collective-permute-done | bytes 32800 | tf_op jit(solution)/shard_map/ppermute | solution.py:322
  93.4 4.2 %collective-permute-start.14 = (f32[64,128]{1,0:T(8,128)S(1)}, f32[64,128]{1,0:T(8,128)S(1)}, u32[]{:S(2)}, u32[]{:S(2)}) collective-permute-start(f32[64,128]{1,0:T(8,128)S(1)} %add.61), channel_id=1, source_target_pairs={{0,64},{64,0},{128,192},{192,128},{1,65},{65,1},{129,193},{193,129... | collective-permute-start | bytes 98312 | tf_op jit(solution)/shard_map/ppermute | solution.py:322
  97.6 1.5 collective-permute-done.14
  99.1 0.0 collective-permute-start.15
  99.1 7.0 %collective-permute-done.15 = f32[64,128]{1,0:T(8,128)S(1)} collective-permute-done((f32[64,128]{1,0:T(8,128)S(1)}, f32[64,128]{1,0:T(8,128)S(1)}, u32[]{:S(2)}, u32[]{:S(2)}) %collective-permute-start.15) | collective-permute-done | bytes 32800 | tf_op jit(solution)/shard_map/ppermute | solution.py:322
  106.1 3.0 %collective-permute-start.16 = (f32[64,128]{1,0:T(8,128)S(1)}, f32[64,128]{1,0:T(8,128)S(1)}, u32[]{:S(2)}, u32[]{:S(2)}) collective-permute-start(f32[64,128]{1,0:T(8,128)S(1)} %add.63), channel_id=1, source_target_pairs={{0,8},{4,12},{8,0},{12,4},{1,9},{5,13},{9,1},{13,5},{2,10},{6,14},... | collective-permute-start | bytes 98312 | tf_op jit(solution)/shard_map/ppermute | solution.py:322
  109.1 1.3 collective-permute-done.16
  110.4 1.2 collective-permute-start.17
  111.6 1.6 copy-done.4
  113.2 5.3 %shard_map.107 = (f32[2,640,512]{2,1,0:T(8,128)}, f32[640,128]{1,0:T(8,128)S(1)}, f32[640,128]{1,0:T(8,128)S(1)}) custom-call(s32[1]{0:T(128)} %bitcast.8.counts, s32[32]{0:T(128)S(1)} %reshape.24.offsets, f32[17,2,128,128]{3,2,1,0:T(8,128)S(1)} %copy-done.3, f32[17,2,128,128]{3,2,1,0:T(8,128)S(1)} %copy-done.4), custom_call_target="tpu_custom_call" | custom-call | tf_op jit(solution)/shard_map/pallas_call | solution.py:306
  118.5 7.8 %collective-permute-start.4 = (f32[640,128]{1,0:T(8,128)S(1)}, f32[640,128]{1,0:T(8,128)S(1)}, u32[]{:S(2)}, u32[]{:S(2)}) collective-permute-start(f32[640,128]{1,0:T(8,128)S(1)} %get-tuple-element.19), channel_id=1, source_target_pairs={{0,1},{1,2},{2,3},{3,4},{4,5},{5,6},{6,7},{7,8},{8,9},{9,10},{10,1... | collective-permute-start | bytes 983048 | tf_op jit(solution)/shard_map/ppermute | solution.py:318
  126.3 6.9 %collective-permute-start.5 = (f32[640,128]{1,0:T(8,128)S(1)}, f32[640,128]{1,0:T(8,128)S(1)}, u32[]{:S(2)}, u32[]{:S(2)}) collective-permute-start(f32[640,128]{1,0:T(8,128)S(1)} %get-tuple-element.20), channel_id=1, source_target_pairs={{1,0},{2,1},{3,2},{4,3},{5,4},{6,5},{7,6},{8,7},{9,8},{10,9},{11,1... | collective-permute-start | bytes 983048 | tf_op jit(solution)/shard_map/ppermute | solution.py:318
  133.3 0.0 collective-permute-done.17
  133.3 2.3 %collective-permute-start.18 = (f32[256,128]{1,0:T(8,128)S(1)}, f32[256,128]{1,0:T(8,128)S(1)}, u32[]{:S(2)}, u32[]{:S(2)}) collective-permute-start(f32[256,128]{1,0:T(8,128)S(1)} %maximum_select_fusion.2), channel_id=1, source_target_pairs={{0,2},{2,0},{1,3},{3,1},{4,6},{6,4},{5,7},{7,5},{8,10},{10,8},{9,1... | collective-permute-start | bytes 393224 | tf_op jit(solution)/shard_map/ppermute | solution.py:322
  135.6 1.1 fusion.1
  136.6 0.0 collective-permute-done.4.from_left
  136.7 0.0 collective-permute-done.5.from_right
  136.7 0.9 shard_map.108
  137.5 7.6 %collective-permute-start.6 = (f32[2,64,512]{2,1,0:T(8,128)}, f32[2,64,512]{2,1,0:T(8,128)S(1)}, u32[]{:S(2)}, u32[]{:S(2)}) collective-permute-start(f32[2,64,512]{2,1,0:T(8,128)} %get-tuple-element.21), channel_id=1, source_target_pairs={{0,16},{16,32},{32,48},{48,64},{64,80},{80,96},{96,112},{112,128},... | collective-permute-start | bytes 786440 | tf_op jit(solution)/shard_map/ppermute | solution.py:318
  145.2 1.9 %collective-permute-start.7 = (f32[2,64,512]{2,1,0:T(8,128)}, f32[2,64,512]{2,1,0:T(8,128)}, u32[]{:S(2)}, u32[]{:S(2)}) collective-permute-start(f32[2,64,512]{2,1,0:T(8,128)} %get-tuple-element.22), channel_id=1, source_target_pairs={{16,0},{32,16},{48,32},{64,48},{80,64},{96,80},{112,96},{128,112},... | collective-permute-start | bytes 786440 | tf_op jit(solution)/shard_map/ppermute | solution.py:318
  147.1 0.0 collective-permute-done.18
  147.1 0.7 maximum_select_fusion.1
  147.8 1.9 %collective-permute-start.19 = (f32[512,128]{1,0:T(8,128)}, f32[512,128]{1,0:T(8,128)}, u32[]{:S(2)}, u32[]{:S(2)}) collective-permute-start(f32[512,128]{1,0:T(8,128)} %maximum_select_fusion.1), channel_id=1, source_target_pairs={{0,1},{1,0},{2,3},{3,2},{4,5},{5,4},{6,7},{7,6},{8,9},{9,8},{10,11... | collective-permute-start | bytes 786440 | tf_op jit(solution)/shard_map/ppermute | solution.py:322
  149.7 1.9 %collective-permute-done.6.from_above = f32[2,64,512]{2,1,0:T(8,128)S(1)} collective-permute-done((f32[2,64,512]{2,1,0:T(8,128)}, f32[2,64,512]{2,1,0:T(8,128)S(1)}, u32[]{:S(2)}, u32[]{:S(2)}) %collective-permute-start.6) | collective-permute-done | bytes 262176 | tf_op jit(solution)/shard_map/ppermute | solution.py:318
  151.6 12.5 %collective-permute-done.7.from_below = f32[2,64,512]{2,1,0:T(8,128)} collective-permute-done((f32[2,64,512]{2,1,0:T(8,128)}, f32[2,64,512]{2,1,0:T(8,128)}, u32[]{:S(2)}, u32[]{:S(2)}) %collective-permute-start.7) | collective-permute-done | bytes 262176 | tf_op jit(solution)/shard_map/ppermute | solution.py:318
  164.0 2.5 %shard_map.109 = f32[2,512,512]{2,1,0:T(8,128)} custom-call(f32[2,640,512]{2,1,0:T(8,128)S(1)} %copy-done.2, f32[640,128]{1,0:T(8,128)S(1)} %collective-permute-done.4.from_left, f32[640,128]{1,0:T(8,128)S(1)} %collective-permute-done.5.from_right, f32[2,64,512]{2,1,0:T(8,128)S(1)} %collective-permute-done.6.from_above, ...), custom_call_target="tpu_custom_call" | custom-call | tf_op jit(solution)/shard_map/pallas_call | solution.py:306
  166.6 0.0 collective-permute-done.19
  166.6 2.0 %fusion = f32[1024,128]{1,0:T(8,128)} fusion(f32[512,128]{1,0:T(8,128)} %collective-permute-done.19, f32[512,128]{1,0:T(8,128)} %maximum_select_fusion.1, pred[]{:T(512)S(6)} %eq.12), kind=kLoop, calls=%fused_computation.1 | loop fusion | flops 524288 | bytes 1048577 | tf_op jit(solution)/shard_map/mul | solution.py:371
  (33 shorter events, 0.2 us)
Async XLA Ops:
  0.6 31.2 %copy-start.6 = (bf16[768,256]{1,0:T(8,128)(2,1)S(1)}, bf16[768,256]{1,0:T(8,128)(2,1)}, u32[]{:S(2)}) copy-start(bf16[768,256]{1,0:T(8,128)(2,1)} %constant.35.clone.rf) | copy-start | bytes 1179652
  0.6 31.2 %copy-start = (f32[2,512,512]{2,1,0:T(8,128)S(1)}, f32[2,512,512]{2,1,0:T(8,128)}, u32[]{:S(2)}) copy-start(f32[2,512,512]{2,1,0:T(8,128)} %tile.3) | copy-start | bytes 6291460
  0.7 30.3 %copy-start.14 = (s32[1,1,16,2]{2,3,1,0:T(2,128)S(1)}, s32[1,1,16,2]{2,3,1,0:T(2,128)}, u32[]{:S(2)}) copy-start(s32[1,1,16,2]{2,3,1,0:T(2,128)} %param.12) | copy-start | bytes 388
  0.7 31.2 %copy-start.1 = (f32[1,1,16,128,128]{4,3,2,1,0:T(8,128)S(1)}, f32[1,1,16,128,128]{4,3,2,1,0:T(8,128)}, u32[]{:S(2)}) copy-start(f32[1,1,16,128,128]{4,3,2,1,0:T(8,128)} %param.11) | copy-start | bytes 3145732
  1.9 9.8 %collective-permute-start = (f32[2,64,512]{2,1,0:T(8,128)S(1)}, f32[2,64,512]{2,1,0:T(8,128)S(1)}, u32[]{:S(2)}, u32[]{:S(2)}) collective-permute-start(f32[2,64,512]{2,1,0:T(8,128)S(1)} %get-tuple-element.29), channel_id=1, source_target_pairs={{0,16},{16,32},{32,48},{48,64},{64,80},{80,96},{96,112},{112,128},... | collective-permute-start | bytes 786440 | tf_op jit(solution)/shard_map/ppermute | solution.py:318
  6.7 17.4 %collective-permute-start.1 = (f32[2,64,512]{2,1,0:T(8,128)S(1)}, f32[2,64,512]{2,1,0:T(8,128)S(1)}, u32[]{:S(2)}, u32[]{:S(2)}) collective-permute-start(f32[2,64,512]{2,1,0:T(8,128)S(1)} %get-tuple-element.28), channel_id=1, source_target_pairs={{16,0},{32,16},{48,32},{64,48},{80,64},{96,80},{112,96},{128,112},... | collective-permute-start | bytes 786440 | tf_op jit(solution)/shard_map/ppermute | solution.py:318
  11.7 13.5 %copy-start.10 = (f32[2,64,512]{2,1,0:T(8,128)}, f32[2,64,512]{2,1,0:T(8,128)S(1)}, u32[]{:S(2)}) copy-start(f32[2,64,512]{2,1,0:T(8,128)S(1)} %collective-permute-done.above) | copy-start | bytes 786436
  24.1 1.1 copy-start.12
  25.2 19.6 %collective-permute-start.2 = (f32[640,128]{1,0:T(8,128)}, f32[640,128]{1,0:T(8,128)}, u32[]{:S(2)}, u32[]{:S(2)}) collective-permute-start(f32[640,128]{1,0:T(8,128)} %get-tuple-element.14), channel_id=1, source_target_pairs={{0,1},{1,2},{2,3},{3,4},{4,5},{5,6},{6,7},{7,8},{8,9},{9,10},{10,1... | collective-permute-start | bytes 983048 | tf_op jit(solution)/shard_map/ppermute | solution.py:318
  27.1 17.7 %collective-permute-start.3 = (f32[640,128]{1,0:T(8,128)}, f32[640,128]{1,0:T(8,128)}, u32[]{:S(2)}, u32[]{:S(2)}) collective-permute-start(f32[640,128]{1,0:T(8,128)} %get-tuple-element.15), channel_id=1, source_target_pairs={{1,0},{2,1},{3,2},{4,3},{5,4},{6,5},{7,6},{8,7},{9,8},{10,9},{11,1... | collective-permute-start | bytes 983048 | tf_op jit(solution)/shard_map/ppermute | solution.py:318
  31.9 1.0 copy-start.5
  32.9 1.0 copy-start.7
  33.9 1.0 copy-start.8
  34.9 1.0 copy-start.9
  35.9 8.9 %copy-start.11 = (f32[2,64,512]{2,1,0:T(8,128)S(1)}, f32[2,64,512]{2,1,0:T(8,128)}, u32[]{:S(2)}) copy-start(f32[2,64,512]{2,1,0:T(8,128)} %copy-done.10) | copy-start | bytes 786436
  35.9 8.9 %copy-start.13 = (f32[2,64,512]{2,1,0:T(8,128)S(1)}, f32[2,64,512]{2,1,0:T(8,128)}, u32[]{:S(2)}) copy-start(f32[2,64,512]{2,1,0:T(8,128)} %copy-done.12) | copy-start | bytes 786436
  55.2 56.4 %copy-start.3 = (f32[17,2,128,128]{3,2,1,0:T(8,128)S(1)}, f32[17,2,128,128]{3,2,1,0:T(8,128)}, u32[]{:S(2)}) copy-start(f32[17,2,128,128]{3,2,1,0:T(8,128)} %get-tuple-element.13.early_grads) | copy-start | bytes 6684676
  56.3 16.3 %collective-permute-start.8 = (f32[512,128]{1,0:T(8,128)S(1)}, f32[512,128]{1,0:T(8,128)S(1)}, u32[]{:S(2)}, u32[]{:S(2)}) collective-permute-start(f32[512,128]{1,0:T(8,128)S(1)} %constant_dynamic-slice_fusion.3), channel_id=1, source_target_pairs={{0,1},{1,0},{2,3},{3,2},{4,5},{5,4},{6,7},{7,6},{8,9},{9,8},{10,11... | collective-permute-start | bytes 786440 | tf_op jit(solution)/shard_map/ppermute | solution.py:322
  73.6 4.8 %collective-permute-start.9 = (f32[256,128]{1,0:T(8,128)S(1)}, f32[256,128]{1,0:T(8,128)S(1)}, u32[]{:S(2)}, u32[]{:S(2)}) collective-permute-start(f32[256,128]{1,0:T(8,128)S(1)} %constant_dynamic-slice_fusion.2), channel_id=1, source_target_pairs={{0,2},{2,0},{1,3},{3,1},{4,6},{6,4},{5,7},{7,5},{8,10},{10,8},{9,1... | collective-permute-start | bytes 393224 | tf_op jit(solution)/shard_map/ppermute | solution.py:322
  78.5 3.2 %collective-permute-start.10 = (f32[128,128]{1,0:T(8,128)S(1)}, f32[128,128]{1,0:T(8,128)S(1)}, u32[]{:S(2)}, u32[]{:S(2)}) collective-permute-start(f32[128,128]{1,0:T(8,128)S(1)} %constant_dynamic-slice_fusion.1), channel_id=1, source_target_pairs={{0,4},{4,0},{8,12},{12,8},{1,5},{5,1},{9,13},{13,9},{2,6},{6,2},{1... | collective-permute-start | bytes 196616 | tf_op jit(solution)/shard_map/ppermute | solution.py:322
  81.7 4.4 %collective-permute-start.11 = (f32[64,128]{1,0:T(8,128)S(1)}, f32[64,128]{1,0:T(8,128)S(1)}, u32[]{:S(2)}, u32[]{:S(2)}) collective-permute-start(f32[64,128]{1,0:T(8,128)S(1)} %constant_dynamic-slice_fusion), channel_id=1, source_target_pairs={{0,8},{4,12},{8,0},{12,4},{1,9},{5,13},{9,1},{13,5},{2,10},{6,14},... | collective-permute-start | bytes 98312 | tf_op jit(solution)/shard_map/ppermute | solution.py:322
  86.1 3.1 %collective-permute-start.12 = (f32[64,128]{1,0:T(8,128)S(1)}, f32[64,128]{1,0:T(8,128)S(1)}, u32[]{:S(2)}, u32[]{:S(2)}) collective-permute-start(f32[64,128]{1,0:T(8,128)S(1)} %dynamic-slice_add_fusion.3), channel_id=1, source_target_pairs={{0,16},{16,0},{32,48},{48,32},{1,17},{17,1},{33,49},{49,33},{2,18}... | collective-permute-start | bytes 98312 | tf_op jit(solution)/shard_map/ppermute | solution.py:322
  89.1 4.3 %collective-permute-start.13 = (f32[64,128]{1,0:T(8,128)S(1)}, f32[64,128]{1,0:T(8,128)S(1)}, u32[]{:S(2)}, u32[]{:S(2)}) collective-permute-start(f32[64,128]{1,0:T(8,128)S(1)} %add.60), channel_id=1, source_target_pairs={{0,32},{16,48},{32,0},{48,16},{1,33},{17,49},{33,1},{49,17},{2,34}... | collective-permute-start | bytes 98312 | tf_op jit(solution)/shard_map/ppermute | solution.py:322
  93.4 5.7 %collective-permute-start.14 = (f32[64,128]{1,0:T(8,128)S(1)}, f32[64,128]{1,0:T(8,128)S(1)}, u32[]{:S(2)}, u32[]{:S(2)}) collective-permute-start(f32[64,128]{1,0:T(8,128)S(1)} %add.61), channel_id=1, source_target_pairs={{0,64},{64,0},{128,192},{192,128},{1,65},{65,1},{129,193},{193,129... | collective-permute-start | bytes 98312 | tf_op jit(solution)/shard_map/ppermute | solution.py:322
  99.1 7.0 %collective-permute-start.15 = (f32[64,128]{1,0:T(8,128)S(1)}, f32[64,128]{1,0:T(8,128)S(1)}, u32[]{:S(2)}, u32[]{:S(2)}) collective-permute-start(f32[64,128]{1,0:T(8,128)S(1)} %add.62), channel_id=1, source_target_pairs={{0,128},{64,192},{128,0},{192,64},{1,129},{65,193},{129,1},{193,65... | collective-permute-start | bytes 98312 | tf_op jit(solution)/shard_map/ppermute | solution.py:322
  106.1 4.3 %collective-permute-start.16 = (f32[64,128]{1,0:T(8,128)S(1)}, f32[64,128]{1,0:T(8,128)S(1)}, u32[]{:S(2)}, u32[]{:S(2)}) collective-permute-start(f32[64,128]{1,0:T(8,128)S(1)} %add.63), channel_id=1, source_target_pairs={{0,8},{4,12},{8,0},{12,4},{1,9},{5,13},{9,1},{13,5},{2,10},{6,14},... | collective-permute-start | bytes 98312 | tf_op jit(solution)/shard_map/ppermute | solution.py:322
  110.4 22.8 %collective-permute-start.17 = (f32[128,128]{1,0:T(8,128)S(1)}, f32[128,128]{1,0:T(8,128)S(1)}, u32[]{:S(2)}, u32[]{:S(2)}) collective-permute-start(f32[128,128]{1,0:T(8,128)S(1)} %maximum_select_fusion.3), channel_id=1, source_target_pairs={{0,4},{4,0},{8,12},{12,8},{1,5},{5,1},{9,13},{13,9},{2,6},{6,2},{1... | collective-permute-start | bytes 196616 | tf_op jit(solution)/shard_map/ppermute | solution.py:322
  111.6 1.6 copy-start.4
  118.5 45.6 %copy-start.2 = (f32[2,640,512]{2,1,0:T(8,128)S(1)}, f32[2,640,512]{2,1,0:T(8,128)}, u32[]{:S(2)}) copy-start(f32[2,640,512]{2,1,0:T(8,128)} %get-tuple-element.18.middle) | copy-start | bytes 7864324
  118.5 18.2 %collective-permute-start.4 = (f32[640,128]{1,0:T(8,128)S(1)}, f32[640,128]{1,0:T(8,128)S(1)}, u32[]{:S(2)}, u32[]{:S(2)}) collective-permute-start(f32[640,128]{1,0:T(8,128)S(1)} %get-tuple-element.19), channel_id=1, source_target_pairs={{0,1},{1,2},{2,3},{3,4},{4,5},{5,6},{6,7},{7,8},{8,9},{9,10},{10,1... | collective-permute-start | bytes 983048 | tf_op jit(solution)/shard_map/ppermute | solution.py:318
  126.3 10.3 %collective-permute-start.5 = (f32[640,128]{1,0:T(8,128)S(1)}, f32[640,128]{1,0:T(8,128)S(1)}, u32[]{:S(2)}, u32[]{:S(2)}) collective-permute-start(f32[640,128]{1,0:T(8,128)S(1)} %get-tuple-element.20), channel_id=1, source_target_pairs={{1,0},{2,1},{3,2},{4,3},{5,4},{6,5},{7,6},{8,7},{9,8},{10,9},{11,1... | collective-permute-start | bytes 983048 | tf_op jit(solution)/shard_map/ppermute | solution.py:318
  133.3 13.8 %collective-permute-start.18 = (f32[256,128]{1,0:T(8,128)S(1)}, f32[256,128]{1,0:T(8,128)S(1)}, u32[]{:S(2)}, u32[]{:S(2)}) collective-permute-start(f32[256,128]{1,0:T(8,128)S(1)} %maximum_select_fusion.2), channel_id=1, source_target_pairs={{0,2},{2,0},{1,3},{3,1},{4,6},{6,4},{5,7},{7,5},{8,10},{10,8},{9,1... | collective-permute-start | bytes 393224 | tf_op jit(solution)/shard_map/ppermute | solution.py:322
  137.5 14.0 %collective-permute-start.6 = (f32[2,64,512]{2,1,0:T(8,128)}, f32[2,64,512]{2,1,0:T(8,128)S(1)}, u32[]{:S(2)}, u32[]{:S(2)}) collective-permute-start(f32[2,64,512]{2,1,0:T(8,128)} %get-tuple-element.21), channel_id=1, source_target_pairs={{0,16},{16,32},{32,48},{48,64},{64,80},{80,96},{96,112},{112,128},... | collective-permute-start | bytes 786440 | tf_op jit(solution)/shard_map/ppermute | solution.py:318
  145.2 18.9 %collective-permute-start.7 = (f32[2,64,512]{2,1,0:T(8,128)}, f32[2,64,512]{2,1,0:T(8,128)}, u32[]{:S(2)}, u32[]{:S(2)}) collective-permute-start(f32[2,64,512]{2,1,0:T(8,128)} %get-tuple-element.22), channel_id=1, source_target_pairs={{16,0},{32,16},{48,32},{64,48},{80,64},{96,80},{112,96},{128,112},... | collective-permute-start | bytes 786440 | tf_op jit(solution)/shard_map/ppermute | solution.py:318
  147.8 18.8 %collective-permute-start.19 = (f32[512,128]{1,0:T(8,128)}, f32[512,128]{1,0:T(8,128)}, u32[]{:S(2)}, u32[]{:S(2)}) collective-permute-start(f32[512,128]{1,0:T(8,128)} %maximum_select_fusion.1), channel_id=1, source_target_pairs={{0,1},{1,0},{2,3},{3,2},{4,5},{5,4},{6,7},{7,6},{8,9},{9,8},{10,11... | collective-permute-start | bytes 786440 | tf_op jit(solution)/shard_map/ppermute | solution.py:322

commit v2 on v1

v2 whole, which is shorter than its diff:
```python
import functools
import math

import jax
import jax.numpy as jnp
import ml_dtypes
import numpy as np
from jax import lax
from jax.experimental import pallas as pl
from jax.experimental.pallas import tpu as pltpu
from jax.sharding import Mesh
from jax.sharding import PartitionSpec as P

PATCH = 128
MODES = 4
TILE = 512
SLOTS = 16
HALF = 64
EXT = TILE + 2 * HALF
BLOCKS = 6
GROUP = 4

ROW = ("zh", "x")
COL = ("y", "zl", "core")


def split_table(table):
    high = table.astype(np.float32).astype(ml_dtypes.bfloat16)
    low = (table - high.astype(np.float64)).astype(np.float32).astype(ml_dtypes.bfloat16)
    return high, low


def dft_tables(n):
    i = np.arange(n)
    angles = (np.outer(i, i) % n) * (2 * math.pi / n)
    cos, sin = np.cos(angles) / math.sqrt(n), -np.sin(angles) / math.sqrt(n)
    forward = np.block([[cos, sin], [-sin, cos]])
    fh, fl = split_table(forward)
    ih, il = split_table(forward.T)
    return np.stack([fh, fl]), np.stack([ih, il])


def split(x):
    high = x.astype(jnp.bfloat16)
    return high, (x - high.astype(jnp.float32)).astype(jnp.bfloat16)


def dot(a, b):
    return jnp.dot(a, b, preferred_element_type=jnp.float32)


def right_dft(x, table):
    high, low = split(x)
    return dot(high, table[0]) + dot(low, table[0]) + dot(high, table[1])


def left_dft(table, x):
    high, low = split(x)
    return dot(table[0], high) + dot(table[1], high) + dot(table[0], low)


def to_cols(y):
    n = PATCH
    return jnp.concatenate(
        [jnp.concatenate([y[m * n : (m + 1) * n, p * n : (p + 1) * n] for m in range(MODES)], 1) for p in range(2)], 0
    )


def to_rows(z):
    n = PATCH
    return jnp.concatenate(
        [jnp.concatenate([z[p * n : (p + 1) * n, m * n : (m + 1) * n] for p in range(2)], 1) for m in range(MODES)], 0
    )


def lane_iota(rows):
    return lax.broadcasted_iota(jnp.int32, (rows, PATCH), 1)


def is_inside(offsets, k):
    r, c = offsets[0, 0, 0, k], offsets[0, 0, 1, k]
    top = TILE - PATCH
    return (r >= 0) & (r <= top) & (c >= 0) & (c <= top)


def early_slots(counts, offsets):
    live = counts[0, 0]

    def tally(k, total):
        return total + jnp.where(is_inside(offsets, k) & (k < live), 1, 0)

    inside = lax.fori_loop(0, SLOTS, tally, 0)
    return live, inside // 2 * 2


def choose_slots(counts, offsets, chosen, early):
    live, first = early_slots(counts, offsets)

    def pick(k, state):
        seen, size = state
        inner = is_inside(offsets, k)
        is_early = inner & (seen < first)
        chosen[size] = k
        take = (is_early == early) & (k < live)
        seen = seen + jnp.where(inner, 1, 0)
        return seen, size + jnp.where(take, 1, 0)

    _, size = lax.fori_loop(0, SLOTS, pick, (0, 0))
    return size


def slot_work(k, out_slot, scale, offsets, extended, amplitudes, probe, tables, patch_grads, probe_total):
    forward, inverse = tables
    n = PATCH
    row = offsets[0, 0, 0, k] + HALF
    col = offsets[0, 0, 1, k] + PATCH
    block = col // n
    lead = col - block * n
    turn = jnp.where(lead == 0, 0, n - lead)
    lane = lane_iota(n)
    parts = []
    for p in range(2):
        a = pltpu.roll(extended[p, block, pl.ds(row, n), :], turn, 1)
        b = pltpu.roll(extended[p, block + 1, pl.ds(row, n), :], turn, 1)
        parts.append(jnp.where(lane < n - lead, a, b))
    obj_r, obj_i = parts
    waves = []
    for m in range(MODES):
        pr, pi = probe[m, 0], probe[m, 1]
        waves.append(jnp.concatenate([pr * obj_r - pi * obj_i, pr * obj_i + pi * obj_r], 1))
    far = left_dft(inverse, to_cols(right_dft(jnp.concatenate(waves, 0), forward)))
    power = far * far
    power = power[:n] + power[n:]
    intensity = power[:, :n] + power[:, n : 2 * n] + power[:, 2 * n : 3 * n] + power[:, 3 * n :]
    measured = amplitudes[k]
    residual = (intensity - measured * measured) * scale
    weighted = far * jnp.concatenate([jnp.concatenate([residual] * MODES, 1)] * 2, 0)
    back = right_dft(to_rows(left_dft(forward, weighted)), inverse)
    total_r = total_i = None
    for m in range(MODES):
        gr, gi = back[m * n : (m + 1) * n, :n], back[m * n : (m + 1) * n, n:]
        pr, pi = probe[m, 0], probe[m, 1]
        tr, ti = pr * gr + pi * gi, pr * gi - pi * gr
        total_r, total_i = (tr, ti) if m == 0 else (total_r + tr, total_i + ti)
        probe_total[m, 0] += obj_r * gr + obj_i * gi
        probe_total[m, 1] += obj_r * gi - obj_i * gr
    patch_grads[out_slot, 0] = total_r
    patch_grads[out_slot, 1] = total_i


def tile_copies(tile, extended, sem):
    return [
        pltpu.make_async_copy(
            tile.at[:, :, pl.ds(b * PATCH, PATCH)], extended.at[:, b + 1, pl.ds(HALF, TILE), :], sem
        )
        for b in range(TILE // PATCH)
    ]


def run_slots(early, counts, offsets, amps, patch_grads, probe_in, probe_total, scratch, copies, others=()):
    extended, measured, probe, grads, forward, inverse, chosen, sem, out_sems = scratch
    copies = copies + [pltpu.make_async_copy(amps, measured, sem), pltpu.make_async_copy(probe_in, probe, sem)]
    for c in copies:
        c.start()
    size = choose_slots(counts, offsets, chosen, early)
    for c in [*copies, *others]:
        c.wait()

    def step(first, count):
        for u in range(count):
            i = first + u
            on = i < size
            k = jnp.where(on, chosen[jnp.minimum(i, SLOTS - 1)], 0)
            out = jnp.where(on, k, SLOTS)
            scale = jnp.where(on, 2.0, 0.0)
            slot_work(k, out, scale, offsets, extended, measured, probe, (forward, inverse), grads, probe_total)
        for u in range(count):
            i = first + u

            @pl.when(i < size)
            def _():
                k = chosen[i]
                pltpu.make_async_copy(grads.at[k], patch_grads.at[k], out_sems.at[k]).start()

    whole = size // GROUP * GROUP

    def group(j, carry):
        step(j * GROUP, GROUP)
        return carry

    def pair(j, carry):
        step(whole + j * 2, 2)
        return carry

    lax.fori_loop(0, size // GROUP, group, 0)
    lax.fori_loop(0, (size - whole + 1) // 2, pair, 0)

    def finish(i, carry):
        k = chosen[i]
        pltpu.make_async_copy(grads.at[k], patch_grads.at[k], out_sems.at[k]).wait()
        return carry

    lax.fori_loop(0, size, finish, 0)


def early_kernel(counts, offsets, tile, amps, probe, forward, inverse, patch_grads, probe_total, *scratch):
    extended, sem = scratch[0], scratch[-2]
    copies = tile_copies(tile, extended, sem) + [
        pltpu.make_async_copy(forward, scratch[4], sem),
        pltpu.make_async_copy(inverse, scratch[5], sem),
    ]
    probe_total[...] = jnp.zeros_like(probe_total)
    run_slots(True, counts, offsets, amps, patch_grads, probe, probe_total, scratch, copies)


def late_kernel(
    counts, offsets, sides, tile, rows_a, rows_b, amps, probe, forward, inverse, cols_a, cols_b, corners_a, corners_b,
    probe_before, patch_grads, probe_total, *scratch
):
    extended, side_sem, sem = scratch[0], scratch[-3], scratch[-2]
    scratch = scratch[:-3] + scratch[-2:]
    copies = tile_copies(tile, extended, sem) + [
        pltpu.make_async_copy(forward, scratch[4], sem),
        pltpu.make_async_copy(inverse, scratch[5], sem),
    ]
    even_row, even_col = sides[0] == 0, sides[1] == 0

    def strip_copies(above, below):
        return [
            pltpu.make_async_copy(
                source.at[:, :, pl.ds(b * PATCH, PATCH)], extended.at[:, b + 1, pl.ds(top, HALF), :], side_sem
            )
            for source, top in ((above, 0), (below, HALF + TILE))
            for b in range(TILE // PATCH)
        ]

    def start(above, below):
        for c in strip_copies(above, below):
            c.start()

    @pl.when(even_row)
    def _():
        start(rows_b, rows_a)

    @pl.when(jnp.logical_not(even_row))
    def _():
        start(rows_a, rows_b)

    probe_total[...] = probe_before[...]

    def columns(left, right, left_corners, right_corners):
        for rows, l, r in (
            (pl.ds(HALF, TILE), left[...], right[...]),
            (pl.ds(0, HALF), left_corners[:HALF, :], right_corners[:HALF, :]),
            (pl.ds(HALF + TILE, HALF), left_corners[HALF:, :], right_corners[HALF:, :]),
        ):
            extended[0, 0, rows, :] = pltpu.roll(l, HALF, 1)
            extended[1, 0, rows, :] = l
            extended[0, BLOCKS - 1, rows, :] = r
            extended[1, BLOCKS - 1, rows, :] = pltpu.roll(r, HALF, 1)

    @pl.when(even_col)
    def _():
        columns(cols_b, cols_a, corners_b, corners_a)

    @pl.when(jnp.logical_not(even_col))
    def _():
        columns(cols_a, cols_b, corners_a, corners_b)

    run_slots(
        False, counts, offsets, amps, patch_grads, probe, probe_total, scratch, copies, strip_copies(rows_a, rows_b)
    )


def put_by_side(even, a, b, after, before):
    @pl.when(even)
    def _():
        a[...] = after
        b[...] = before

    @pl.when(jnp.logical_not(even))
    def _():
        a[...] = before
        b[...] = after


def pack_kernel(sides, tile, cols_a, cols_b, first, last, sem):
    copies = [
        pltpu.make_async_copy(tile.at[:, :, pl.ds(0, PATCH)], first, sem),
        pltpu.make_async_copy(tile.at[:, :, pl.ds(TILE - PATCH, PATCH)], last, sem),
    ]
    for c in copies:
        c.start()
    for c in copies:
        c.wait()
    low = lane_iota(TILE) < HALF
    put_by_side(
        sides[1] == 0,
        cols_a,
        cols_b,
        jnp.where(low, pltpu.roll(last[0], HALF, 1), last[1]),
        jnp.where(low, first[0], pltpu.roll(first[1], HALF, 1)),
    )


def pack_corners_kernel(sides, rows_a, rows_b, corners_a, corners_b, first, last, sem):
    even_row = sides[0] == 0
    copies = []
    for i, source in enumerate((rows_a, rows_b)):
        copies.append(pltpu.make_async_copy(source.at[:, :, pl.ds(0, PATCH)], first.at[i], sem))
        copies.append(pltpu.make_async_copy(source.at[:, :, pl.ds(TILE - PATCH, PATCH)], last.at[i], sem))
    for c in copies:
        c.start()
    for c in copies:
        c.wait()
    low = lane_iota(HALF) < HALF
    for i in range(2):
        l = jnp.where(even_row, first[1 - i], first[i])
        r = jnp.where(even_row, last[1 - i], last[i])
        rows = pl.ds(i * HALF, HALF)
        put_by_side(
            sides[1] == 0,
            corners_a.at[rows, :],
            corners_b.at[rows, :],
            jnp.where(low, pltpu.roll(r[0], HALF, 1), r[1]),
            jnp.where(low, l[0], pltpu.roll(l[1], HALF, 1)),
        )


def deposit_kernel(
    counts, offsets, sides, early_grads, late_grads, inner, rows_a, rows_b, cols_a, cols_b, total, held, flank, sems, out_sem
):
    n = PATCH
    live, first = early_slots(counts, offsets)

    def fetch(k, seen):
        inside = is_inside(offsets, k)
        is_early = inside & (seen < first)

        @pl.when(is_early)
        def _():
            pltpu.make_async_copy(early_grads.at[k], held.at[k], sems.at[k]).start()

        @pl.when(jnp.logical_not(is_early))
        def _():
            pltpu.make_async_copy(late_grads.at[k], held.at[k], sems.at[k]).start()

        return seen + jnp.where(inside, 1, 0)

    lax.fori_loop(0, live, fetch, 0)
    total[...] = jnp.zeros_like(total)
    lane = lane_iota(n)

    def turned(k):
        lead = (offsets[0, 0, 1, k] + n) % n
        pltpu.make_async_copy(early_grads.at[k], held.at[k], sems.at[k]).wait()
        return [pltpu.roll(held[k, p], lead, 1) for p in range(2)]

    def add(k, parts):
        row = offsets[0, 0, 0, k] + HALF
        col = offsets[0, 0, 1, k] + n
        block = col // n
        lead = col - block * n
        rows = pl.ds(row, n)
        old = [[total[p, block + i, rows, :] for i in range(2)] for p in range(2)]
        for p in range(2):
            total[p, block, rows, :] = old[p][0] + jnp.where(lane >= lead, parts[p], 0.0)
            total[p, block + 1, rows, :] = old[p][1] + jnp.where(lane < lead, parts[p], 0.0)

    def add_two(j, carry):
        one, two = turned(2 * j), turned(2 * j + 1)
        add(2 * j, one)
        add(2 * j + 1, two)
        return carry

    lax.fori_loop(0, live // 2, add_two, 0)

    @pl.when(live % 2 == 1)
    def _():
        add(live - 1, turned(live - 1))

    low = lane_iota(EXT) < HALF
    for p in range(2):
        flank[p] = pltpu.roll(jnp.where(low, total[p, BLOCKS - 1], total[p, 0]), HALF, 1)

    def copies(above, below):
        made = []
        for start, rows, out in ((0, HALF, above), (HALF, TILE, inner), (HALF + TILE, HALF, below)):
            for b in range(TILE // n):
                made.append((total.at[:, b + 1, pl.ds(start, rows), :], out.at[:, :, pl.ds(b * n, n)]))
        made.append((flank.at[:, pl.ds(0, HALF), :], above.at[:, :, pl.ds(TILE, n)]))
        made.append((flank.at[:, pl.ds(HALF + TILE, HALF), :], below.at[:, :, pl.ds(TILE, n)]))
        return [pltpu.make_async_copy(near, far, out_sem) for near, far in made]

    def start(above, below):
        for c in copies(above, below):
            c.start()

    @pl.when(sides[0] == 0)
    def _():
        start(rows_b, rows_a)

    @pl.when(sides[0] != 0)
    def _():
        start(rows_a, rows_b)

    low = lane_iota(TILE) < HALF
    own = flank[0, HALF : HALF + TILE, :], flank[1, HALF : HALF + TILE, :]
    put_by_side(
        sides[1] == 0,
        cols_a,
        cols_b,
        jnp.where(low, pltpu.roll(own[0], HALF, 1), own[1]),
        jnp.where(low, own[0], pltpu.roll(own[1], HALF, 1)),
    )
    for c in copies(rows_a, rows_b):
        c.wait()


def corner_kernel(sides, rows_a, rows_b, corners_a, corners_b, held, sem):
    even_row = sides[0] == 0
    copies = [pltpu.make_async_copy(r.at[:, :, pl.ds(TILE, PATCH)], held.at[i], sem) for i, r in enumerate((rows_a, rows_b))]
    for c in copies:
        c.start()
    for c in copies:
        c.wait()
    low = lane_iota(HALF) < HALF
    a, b = held[0], held[1]
    for i, part in enumerate((jnp.where(even_row, b, a), jnp.where(even_row, a, b))):
        rows = pl.ds(i * HALF, HALF)
        put_by_side(
            sides[1] == 0,
            corners_a.at[rows, :],
            corners_b.at[rows, :],
            jnp.where(low, pltpu.roll(part[0], HALF, 1), part[1]),
            jnp.where(low, part[0], pltpu.roll(part[1], HALF, 1)),
        )


def merge_kernel(
    sides, inner, rows_a, rows_b, cols_a, cols_b, corners_a, corners_b, out, left, right, top, bottom, strips, sems, sem
):
    end = TILE - PATCH
    regions = (
        (out.at[:, :, pl.ds(0, PATCH)], left),
        (out.at[:, :, pl.ds(end, PATCH)], right),
        (out.at[:, pl.ds(0, HALF), pl.ds(PATCH, TILE - 2 * PATCH)], top),
        (out.at[:, pl.ds(TILE - HALF, HALF), pl.ds(PATCH, TILE - 2 * PATCH)], bottom),
    )
    loads = [pltpu.make_async_copy(far, near, sems.at[i]) for i, (far, near) in enumerate(regions)]
    loads += [pltpu.make_async_copy(r.at[:, :, pl.ds(0, TILE)], strips.at[i], sem) for i, r in enumerate((rows_a, rows_b))]
    for c in loads:
        c.start()
    even_row, even_col = sides[0] == 0, sides[1] == 0

    def both_sides(a, b):
        low = lane_iota(a.shape[0]) < HALF
        from_left, from_right = jnp.where(even_col, b, a), jnp.where(even_col, a, b)
        first = (jnp.where(low, from_left, 0.0), jnp.where(low, pltpu.roll(from_left, HALF, 1), 0.0))
        last = (jnp.where(low, 0.0, pltpu.roll(from_right, HALF, 1)), jnp.where(low, 0.0, from_right))
        return first, last

    sides_terms = both_sides(cols_a[...], cols_b[...])
    corner_terms = both_sides(corners_a[...], corners_b[...])
    for c in loads:
        c.wait()
    a, b = strips[0], strips[1]
    above, below = jnp.where(even_row, b, a), jnp.where(even_row, a, b)
    middle = slice(PATCH, end)
    for p in range(2):
        for i, (near, lanes) in enumerate(((left, slice(0, PATCH)), (right, slice(end, TILE)))):
            near[p] += sides_terms[i][p]
            near[p, :HALF, :] += above[p, :, lanes] + corner_terms[i][p][:HALF]
            near[p, TILE - HALF :, :] += below[p, :, lanes] + corner_terms[i][p][HALF:]
        top[p] += above[p, :, middle]
        bottom[p] += below[p, :, middle]
    stores = [pltpu.make_async_copy(near, far, sems.at[i]) for i, (far, near) in enumerate(regions)]
    for c in stores:
        c.start()
    for c in stores:
        c.wait()


VMEM = pl.BlockSpec(memory_space=pltpu.VMEM)
SMEM = pl.BlockSpec(memory_space=pltpu.SMEM)
HBM = pl.BlockSpec(memory_space=pltpu.HBM)


def call(kernel, in_specs, out_specs, out_shapes, scratch, *args, aliases=None, limit=62):
    return pl.pallas_call(
        kernel,
        in_specs=in_specs,
        out_specs=out_specs,
        out_shape=[jax.ShapeDtypeStruct(s, jnp.float32) for s in out_shapes],
        scratch_shapes=scratch,
        input_output_aliases=aliases or {},
        compiler_params=pltpu.CompilerParams(vmem_limit_bytes=limit * 2**20),
    )(*args)


def swap(value, axes, size, first):
    pairs = [(i, i + 1) for i in range(first, size - 1, 2)]
    return lax.ppermute(value, axes, pairs + [(j, i) for i, j in pairs])


def halve(x, axis):
    half, me = x.shape[0] // 2, lax.axis_index(axis)
    sent = lax.dynamic_slice_in_dim(x, (1 - me) * half, half, 0)
    return lax.dynamic_slice_in_dim(x, me * half, half, 0) + swap(sent, axis, 2, 0)


def double(x, axis):
    other, me = swap(x, axis, 2, 0), lax.axis_index(axis)
    return jnp.where(me == 0, jnp.concatenate([x, other], 0), jnp.concatenate([other, x], 0))


def deal(x, axes, sizes):
    count = math.prod(sizes[a] for a in axes)
    return lax.all_to_all(x.reshape(count, -1, PATCH), axes, 0, 0, tiled=True)


def spread(x, axes, sizes):
    count = math.prod(sizes[a] for a in axes)
    return lax.all_to_all(jnp.broadcast_to(x[None], (count, *x.shape)), axes, 0, 0, tiled=True)


def per_device(sizes, tile, probe, amplitudes, offsets, counts):
    rows, cols = sizes["zh"] * sizes["x"], sizes["y"] * sizes["zl"] * sizes["core"]
    forward, inverse = [jnp.asarray(t) for t in dft_tables(PATCH)]
    offsets = offsets.transpose(0, 1, 3, 2)
    amps = amplitudes.reshape(SLOTS, PATCH, PATCH)
    odd_row, odd_col = lax.axis_index(ROW) % 2, lax.axis_index(COL) % 2
    sides = jnp.stack([odd_row, odd_col]).astype(jnp.int32)
    wide = 2 * PATCH
    slot_scratch = [
        pltpu.VMEM((2, BLOCKS, EXT, PATCH), jnp.float32),
        pltpu.VMEM((SLOTS, PATCH, PATCH), jnp.float32),
        pltpu.VMEM((MODES, 2, PATCH, PATCH), jnp.float32),
        pltpu.VMEM((SLOTS + 1, 2, PATCH, PATCH), jnp.float32),
        pltpu.VMEM((2, wide, wide), jnp.bfloat16),
        pltpu.VMEM((2, wide, wide), jnp.bfloat16),
        pltpu.SMEM((SLOTS + 1,), jnp.int32),
        pltpu.SemaphoreType.DMA,
        pltpu.SemaphoreType.DMA((SLOTS,)),
    ]
    grads_shape, probe_shape = (SLOTS, 2, PATCH, PATCH), (MODES, 2, PATCH, PATCH)
    wide_row, column = (2, HALF, TILE + PATCH), (TILE, PATCH)
    block = pltpu.VMEM((2, TILE, PATCH), jnp.float32)
    low, high = 0, TILE - HALF
    after = lax.dynamic_slice_in_dim(tile, jnp.where(odd_row == 0, high, low), HALF, 1)
    before = lax.dynamic_slice_in_dim(tile, jnp.where(odd_row == 0, low, high), HALF, 1)
    rows_b = swap(before, ROW, rows, 1)
    rows_a = swap(after, ROW, rows, 0)
    cols_a, cols_b = call(
        pack_kernel, [SMEM, HBM], [VMEM] * 2, [column] * 2, [block, block, pltpu.SemaphoreType.DMA], sides, tile, limit=16
    )
    cols_b = swap(cols_b, COL, cols, 1)
    cols_a = swap(cols_a, COL, cols, 0)
    early_grads, probe_early = call(
        early_kernel, [SMEM] * 2 + [HBM] * 5, [HBM, VMEM], [grads_shape, probe_shape], slot_scratch,
        counts, offsets, tile, amps, probe, forward, inverse
    )
    rows_a, rows_b, probe_early = lax.optimization_barrier((rows_a, rows_b, probe_early))
    piece = pltpu.VMEM((2, 2, HALF, PATCH), jnp.float32)
    corners_a, corners_b = call(
        pack_corners_kernel, [SMEM] + [HBM] * 2, [VMEM] * 2, [(PATCH, PATCH)] * 2, [piece, piece, pltpu.SemaphoreType.DMA],
        sides, rows_a, rows_b, limit=16
    )
    corners_b = swap(corners_b, COL, cols, 1)
    corners_a = swap(corners_a, COL, cols, 0)
    late_scratch = slot_scratch[:-2] + [pltpu.SemaphoreType.DMA] + slot_scratch[-2:]
    late_grads, probe_total = call(
        late_kernel, [SMEM] * 3 + [HBM] * 7 + [VMEM] * 5, [HBM, VMEM], [grads_shape, probe_shape], late_scratch,
        counts, offsets, sides, tile, rows_a, rows_b, amps, probe, forward, inverse, cols_a, cols_b, corners_a, corners_b, probe_early
    )

    sums = halve(probe_total.reshape(-1, PATCH), "core")
    inner, rows_a, rows_b, cols_a, cols_b = call(
        deposit_kernel, [SMEM] * 3 + [HBM] * 2, [HBM] * 3 + [VMEM] * 2,
        [(2, TILE, TILE), wide_row, wide_row, column, column],
        [
            pltpu.VMEM((2, BLOCKS, EXT, PATCH), jnp.float32),
            pltpu.VMEM(grads_shape, jnp.float32),
            pltpu.VMEM((2, EXT, PATCH), jnp.float32),
            pltpu.SemaphoreType.DMA((SLOTS,)),
            pltpu.SemaphoreType.DMA,
        ],
        counts, offsets, sides, early_grads, late_grads
    )
    rows_b = swap(rows_b, ROW, rows, 1)
    cols_b = swap(cols_b, COL, cols, 1)
    rows_a = swap(rows_a, ROW, rows, 0)
    cols_a = swap(cols_a, COL, cols, 0)
    plane, line = ("x", "y"), ("zh", "zl")
    sums = jnp.sum(deal(sums, plane, sizes), 0)
    sums = jnp.sum(spread(sums, line, sizes), 0)
    sums, rows_a, rows_b, cols_a, cols_b = lax.optimization_barrier((sums, rows_a, rows_b, cols_a, cols_b))
    corners_a, corners_b = call(
        corner_kernel, [SMEM] + [HBM] * 2, [VMEM] * 2, [(PATCH, PATCH)] * 2, [piece, pltpu.SemaphoreType.DMA],
        sides, rows_a, rows_b, limit=16
    )
    corners_b = swap(corners_b, COL, cols, 1)
    corners_a = swap(corners_a, COL, cols, 0)
    sums = spread(sums, plane, sizes).reshape(-1, PATCH)
    sums, corners_a, corners_b = lax.optimization_barrier((sums, corners_a, corners_b))
    end = pltpu.VMEM((2, HALF, TILE - 2 * PATCH), jnp.float32)
    (object_grad,) = call(
        merge_kernel, [SMEM] + [HBM] * 3 + [VMEM] * 4, [HBM], [(2, TILE, TILE)],
        [block, block, end, end, pltpu.VMEM((2, 2, HALF, TILE), jnp.float32), pltpu.SemaphoreType.DMA((4,)), pltpu.SemaphoreType.DMA],
        sides, inner, rows_a, rows_b, cols_a, cols_b, corners_a, corners_b, aliases={1: 0}, limit=16
    )
    factor = 1.0 / math.sqrt(rows * cols * SLOTS)
    probe_grad = (double(sums, "core") * factor).reshape(probe_shape)
    return object_grad, probe_grad


def solution(mesh):
    sizes = {"zh": 4, "x": 4, "y": 4, "zl": 2, "core": 2}
    fine = Mesh(mesh.devices.reshape(tuple(sizes.values())), tuple(sizes))
    return jax.shard_map(
        functools.partial(per_device, sizes),
        mesh=fine,
        in_specs=(P(None, ROW, COL), P(), P(ROW, COL), P(ROW, COL), P(ROW, COL)),
        out_specs=(P(None, ROW, COL), P()),
        check_vma=False,
    )
```

time: 168 us -> 124 us (0.74); the launches traced: 169 us -> 122 us
  waiting for transfers between devices: 58.8 us -> 7.98 us
  blocking collectives: 0 us -> 16.5 us
  Pallas kernels: 29 us -> 22.5 us
  local copies, waits for them, and re-layouts: 10.6 us -> 5.02 us
    ppermute x20 -> x14, waiting for transfers between devices: 58.8 us -> 7.98 us  [swap(): return lax.ppermute(value, axes, pairs + [(j, i) for i, j in pairs])]
    all_to_all x0 -> x1, blocking collectives: none -> 16.5 us  [spread(): lax.all_to_all(jnp.broadcast_to(x[None], (count, *x.shape)), axes, 0, 0,...]
    all_to_all x0 -> x2, starting transfers between devices: none -> 12.3 us  [the longest x1 6.71 us: deal(): return lax.all_to_all(x.reshape(count, -1, PATCH), axes, 0, 0, tiled=True)]
    ppermute x20 -> x14, starting transfers between devices: 64.7 us -> 53.4 us  [swap(): return lax.ppermute(value, axes, pairs + [(j, i) for i, j in pairs])]
    pallas_call x6 -> x7, Pallas kernels: 29 us -> 22.5 us  [call(): pl.pallas_call(kernel, in_specs=in_specs, out_specs=out_specs, out_shape=...]
    slice x3 -> x0, local copies, waits for them, and re-layouts: 3.57 us -> none  [the longest x1 1.28 us: per_device(): tile[:, :, TILE - PATCH:]]
    unnamed x31 -> x16, local copies, waits for them, and re-layouts: 5.78 us -> 2.23 us
  transfers between devices with their start and end apart: 20 -> 16, of which waited for: 13 -> 3; matrix products, arithmetic and copies ran while one was open for 2% -> 0% of each run, Pallas kernels for 10% -> 11%
where the time goes in v2:
time: 124 us; the launch traced here: 122 us
  starting transfers between devices  65.7 us (53%)
  Pallas kernels  22.5 us (18%)
  blocking collectives  16.5 us (13%)
  waiting for transfers between devices  7.98 us (6%)
  local copies, waits for them, and re-layouts  5.02 us (4%)
  other arithmetic  2.66 us (2%)
  between operations  1.62 us (1%)
    ppermute x14, starting transfers between devices, swap(): return lax.ppermute(value, axes, pairs + [(j, i) for i, j in pairs])  53.4 us
    pallas_call x7, Pallas kernels, call(): pl.pallas_call(kernel, in_specs=in_specs, out_specs=out_specs, out_shape=...  22.5 us
    all_to_all x1, blocking collectives, spread(): lax.all_to_all(jnp.broadcast_to(x[None], (count, *x.shape)), axes, 0, 0,...  16.5 us
    ppermute x14, waiting for transfers between devices, swap(): return lax.ppermute(value, axes, pairs + [(j, i) for i, j in pairs])  7.98 us
    all_to_all x1, starting transfers between devices, deal(): return lax.all_to_all(x.reshape(count, -1, PATCH), axes, 0, 0, tiled=True)  6.71 us
    all_to_all x1, starting transfers between devices, spread(): lax.all_to_all(jnp.broadcast_to(x[None], (count, *x.shape)), axes, 0, 0,...  5.64 us
  transfers between devices with their start and end apart: 16, of which 3 were waited for; matrix products, arithmetic and copies ran while one was open for 0% of the time, Pallas kernels for 11%

profile of v2, /device:TPU:15, one launch (start us, length us, event | category | flops | bytes accessed | tf_op | source)
XLA Modules:
  0.0 121.9 jit_solution(18139377547390209877)
XLA Ops:
  0.6 1.1 constant_dynamic-slice_fusion.1
  1.7 0.6 collective-permute-start
  2.4 5.5 %collective-permute-start.1 = (f32[2,64,512]{2,1,0:T(8,128)S(1)}, f32[2,64,512]{2,1,0:T(8,128)S(1)}, u32[]{:S(2)}, u32[]{:S(2)}) collective-permute-start(f32[2,64,512]{2,1,0:T(8,128)S(1)} %get-tuple-element.54), channel_id=1, source_target_pairs={{16,32},{48,64},{80,96},{112,128},{144,160},{176,192},{208,224},{3... | collective-permute-start | bytes 786440 | tf_op jit(solution)/shard_map/ppermute | solution.py:503
  7.9 0.1 pad_add_fusion.sides
  7.9 0.0 copy-start
  7.9 1.6 %copy-done = f32[2,512,512]{2,1,0:T(8,128)S(1)} copy-done((f32[2,512,512]{2,1,0:T(8,128)S(1)}, f32[2,512,512]{2,1,0:T(8,128)}, u32[]{:S(2)}) %copy-start) | copy-done | bytes 2097176
  9.5 0.0 copy-start.3
  9.5 0.9 shard_map.87
  10.5 1.3 %collective-permute-start.2 = (f32[512,128]{1,0:T(8,128)S(1)}, f32[512,128]{1,0:T(8,128)S(1)}, u32[]{:S(2)}, u32[]{:S(2)}) collective-permute-start(f32[512,128]{1,0:T(8,128)S(1)} %get-tuple-element.32), channel_id=1, source_target_pairs={{0,1},{2,3},{4,5},{6,7},{8,9},{10,11},{12,13},{14,15},{1,0},{3,2},... | collective-permute-start | bytes 786440 | tf_op jit(solution)/shard_map/ppermute | solution.py:503
  11.8 3.4 %collective-permute-start.3 = (f32[512,128]{1,0:T(8,128)S(1)}, f32[512,128]{1,0:T(8,128)}, u32[]{:S(2)}, u32[]{:S(2)}) collective-permute-start(f32[512,128]{1,0:T(8,128)S(1)} %get-tuple-element.33), channel_id=1, source_target_pairs={{1,2},{3,4},{5,6},{7,8},{9,10},{11,12},{13,14},{2,1},{4,3},{6,5},{... | collective-permute-start | bytes 786440 | tf_op jit(solution)/shard_map/ppermute | solution.py:503
  15.9 3.8 %shard_map.86 = (f32[16,2,128,128]{3,2,1,0:T(8,128)}, f32[4,2,128,128]{3,2,1,0:T(8,128)}) custom-call(s32[1,1]{1,0:T(1,128)S(6)} %copy.11.counts, s32[1,1,2,16]{3,2,1,0:T(2,128)} %bitcast.15, f32[2,512,512]{2,1,0:T(8,128)} %tile.5, f32[16,128,128]{2,1,0:T(8,128)} %bitcast.8, f32[4,2,128,128]{3,2,1,0:T(8,128)} %probe.3, ...), custom_call_target="tpu_custom_call" | custom-call | tf_op jit(solution)/shard_map/pallas_call | solution.py:490
  19.7 0.0 collective-permute-done.rows_a
  19.7 0.0 copy-start.1
  19.7 0.0 collective-permute-done.1.rows_b
  19.8 0.0 copy-start.2
  19.8 0.0 copy-done.3
  19.8 0.8 shard_map.88
  20.6 9.5 %collective-permute-start.4 = (f32[128,128]{1,0:T(8,128)S(1)}, f32[128,128]{1,0:T(8,128)S(1)}, u32[]{:S(2)}, u32[]{:S(2)}) collective-permute-start(f32[128,128]{1,0:T(8,128)S(1)} %get-tuple-element.34), channel_id=1, source_target_pairs={{0,1},{2,3},{4,5},{6,7},{8,9},{10,11},{12,13},{14,15},{1,0},{3,2},... | collective-permute-start | bytes 196616 | tf_op jit(solution)/shard_map/ppermute | solution.py:503
  30.1 1.9 %collective-permute-start.5 = (f32[128,128]{1,0:T(8,128)S(1)}, f32[128,128]{1,0:T(8,128)S(1)}, u32[]{:S(2)}, u32[]{:S(2)}) collective-permute-start(f32[128,128]{1,0:T(8,128)S(1)} %get-tuple-element.35), channel_id=1, source_target_pairs={{1,2},{3,4},{5,6},{7,8},{9,10},{11,12},{13,14},{2,1},{4,3},{6,5},{... | collective-permute-start | bytes 196616 | tf_op jit(solution)/shard_map/ppermute | solution.py:503
  32.0 0.0 collective-permute-done.2.cols_a
  32.0 0.0 copy-start.5
  32.0 0.0 collective-permute-done.3.cols_b
  32.0 0.0 collective-permute-done.4.corners_a
  32.0 0.0 copy-start.6
  32.1 3.9 %collective-permute-done.5.corners_b = f32[128,128]{1,0:T(8,128)S(1)} collective-permute-done((f32[128,128]{1,0:T(8,128)S(1)}, f32[128,128]{1,0:T(8,128)S(1)}, u32[]{:S(2)}, u32[]{:S(2)}) %collective-permute-start.5) | collective-permute-done | bytes 65568 | tf_op jit(solution)/shard_map/ppermute | solution.py:503
  36.0 0.0 copy-done.1
  36.0 0.0 copy-done.2
  36.0 0.0 copy-done.5
  36.0 0.0 copy-done.6
  36.0 0.0 copy-start.7
  36.0 0.6 copy-done.7
  36.6 8.5 %shard_map.89 = (f32[16,2,128,128]{3,2,1,0:T(8,128)}, f32[4,2,128,128]{3,2,1,0:T(8,128)}) custom-call(s32[1,1]{1,0:T(1,128)S(6)} %copy.11.counts, s32[1,1,2,16]{3,2,1,0:T(2,128)} %bitcast.16, s32[2]{0:T(128)} %copy-done.3, f32[2,512,512]{2,1,0:T(8,128)} %tile.5, f32[2,64,512]{2,1,0:T(8,128)} %copy-done.1, f32[2,64,512]{2,1,0:T(8,128)} %copy-done.2, ...), custom_call_target="tpu_custom_call" | custom-call | tf_op jit(solution)/shard_map/pallas_call | solution.py:490
  45.1 1.0 constant_dynamic-slice_fusion
  46.0 0.8 collective-permute-start.6
  46.8 1.2 collective-permute-done.6
  48.0 1.7 %dynamic-slice_add_fusion = f32[512,128]{1,0:T(8,128)} fusion(f32[512,128]{1,0:T(8,128)S(1)} %collective-permute-done.6, f32[1024,128]{1,0:T(8,128)} %bitcast.13, s32[]{:T(128)S(6)} %select_n.40), kind=kLoop, calls=%fused_computation.2 | loop fusion | flops 65536 | bytes 786436 | tf_op jit(solution)/shard_map/add | solution.py:509
  49.7 6.7 %all-to-all-start = ((f32[16,32,128]{2,1,0:T(8,128)}), f32[16,32,128]{2,1,0:T(8,128)S(1)}, u32[]{:S(2)}, u32[]{:S(2)}) async-start(f32[16,32,128]{2,1,0:T(8,128)} %bitcast.5), calls=%async_computation | async-start | bytes 524288 | tf_op jit(solution)/shard_map/all_to_all | solution.py:519
  56.4 0.0 copy-start.4
  56.4 4.7 %shard_map.90 = (f32[2,512,512]{2,1,0:T(8,128)}, f32[2,64,640]{2,1,0:T(8,128)}, f32[2,64,640]{2,1,0:T(8,128)}, f32[512,128]{1,0:T(8,128)}, f32[512,128]{1,0:T(8,128)}) custom-call(s32[1,1]{1,0:T(1,128)S(6)} %copy.11.counts, s32[1,1,2,16]{3,2,1,0:T(2,128)} %bitcast.17, s32[2]{0:T(128)} %copy-done.3, f32[16,2,128,128]{3,2,1,0:T(8,128)} %get-tuple-element.28.early_grads, ...), custom_call_target="tpu_custom_call" | custom-call | tf_op jit(solution)/shard_map/pallas_call | solution.py:490
  61.1 1.3 %collective-permute-start.7 = (f32[2,64,640]{2,1,0:T(8,128)}, f32[2,64,640]{2,1,0:T(8,128)S(1)}, u32[]{:S(2)}, u32[]{:S(2)}) collective-permute-start(f32[2,64,640]{2,1,0:T(8,128)} %get-tuple-element.40), channel_id=1, source_target_pairs={{0,16},{32,48},{64,80},{96,112},{128,144},{160,176},{192,208},{224... | collective-permute-start | bytes 983048 | tf_op jit(solution)/shard_map/ppermute | solution.py:503
  62.4 15.8 %collective-permute-start.8 = (f32[2,64,640]{2,1,0:T(8,128)}, f32[2,64,640]{2,1,0:T(8,128)S(1)}, u32[]{:S(2)}, u32[]{:S(2)}) collective-permute-start(f32[2,64,640]{2,1,0:T(8,128)} %get-tuple-element.41), channel_id=1, source_target_pairs={{16,32},{48,64},{80,96},{112,128},{144,160},{176,192},{208,224},{3... | collective-permute-start | bytes 983048 | tf_op jit(solution)/shard_map/ppermute | solution.py:503
  78.1 5.3 %collective-permute-start.10 = (f32[512,128]{1,0:T(8,128)}, f32[512,128]{1,0:T(8,128)S(1)}, u32[]{:S(2)}, u32[]{:S(2)}) collective-permute-start(f32[512,128]{1,0:T(8,128)} %get-tuple-element.43), channel_id=1, source_target_pairs={{1,2},{3,4},{5,6},{7,8},{9,10},{11,12},{13,14},{2,1},{4,3},{6,5},{... | collective-permute-start | bytes 786440 | tf_op jit(solution)/shard_map/ppermute | solution.py:503
  83.5 0.1 collective-permute-start.9
  83.6 0.0 all-to-all-done
  83.7 16.5 %all_to_all.15 = f32[8,32,128]{2,1,0:T(8,128)S(1)} all-to-all(f32[8,32,128]{2,1,0:T(8,128)S(1)} %broadcast_in_dim.4), channel_id=1, replica_groups=mesh['zh'=4,'x'=4,'y'=4,'zl'=2,'core'=2] {'zh','zl'}, dimensions={0} | all-to-all | bytes 262144 | tf_op jit(solution)/shard_map/all_to_all | solution.py:524
  100.1 0.0 collective-permute-done.10.cols_b
  100.1 0.0 collective-permute-done.9.cols_a
  100.2 0.0 collective-permute-done.7.rows_a
  100.2 0.0 collective-permute-done.8.rows_b
  100.2 0.7 broadcast_in_dim.5
  100.9 5.6 %all-to-all-start.2 = ((f32[16,32,128]{2,1,0:T(8,128)}), f32[16,32,128]{2,1,0:T(8,128)S(1)}, u32[]{:S(2)}, u32[]{:S(2)}) async-start(f32[16,32,128]{2,1,0:T(8,128)} %broadcast_in_dim.5), calls=%async_computation.2 | async-start | bytes 524288 | tf_op jit(solution)/shard_map/all_to_all | solution.py:524
  106.5 0.0 copy-done.4
  106.6 0.7 shard_map.91
  107.3 3.5 %collective-permute-start.11 = (f32[128,128]{1,0:T(8,128)S(1)}, f32[128,128]{1,0:T(8,128)S(1)}, u32[]{:S(2)}, u32[]{:S(2)}) collective-permute-start(f32[128,128]{1,0:T(8,128)S(1)} %get-tuple-element.49), channel_id=1, source_target_pairs={{0,1},{2,3},{4,5},{6,7},{8,9},{10,11},{12,13},{14,15},{1,0},{3,2},... | collective-permute-start | bytes 196616 | tf_op jit(solution)/shard_map/ppermute | solution.py:503
  110.8 3.9 %collective-permute-start.12 = (f32[128,128]{1,0:T(8,128)S(1)}, f32[128,128]{1,0:T(8,128)S(1)}, u32[]{:S(2)}, u32[]{:S(2)}) collective-permute-start(f32[128,128]{1,0:T(8,128)S(1)} %get-tuple-element.50), channel_id=1, source_target_pairs={{1,2},{3,4},{5,6},{7,8},{9,10},{11,12},{13,14},{2,1},{4,3},{6,5},{... | collective-permute-start | bytes 196616 | tf_op jit(solution)/shard_map/ppermute | solution.py:503
  114.7 0.0 collective-permute-done.11.corners_a
  114.7 2.9 %collective-permute-done.12.corners_b = f32[128,128]{1,0:T(8,128)S(1)} collective-permute-done((f32[128,128]{1,0:T(8,128)S(1)}, f32[128,128]{1,0:T(8,128)S(1)}, u32[]{:S(2)}, u32[]{:S(2)}) %collective-permute-start.12) | collective-permute-done | bytes 65568 | tf_op jit(solution)/shard_map/ppermute | solution.py:503
  117.6 0.0 all-to-all-done.2
  117.6 0.4 collective-permute-start.13
  118.0 3.1 %shard_map.92 = f32[2,512,512]{2,1,0:T(8,128)} custom-call(s32[2]{0:T(128)S(1)} %copy-done.4, f32[2,512,512]{2,1,0:T(8,128)} %get-tuple-element.38.inner, f32[2,64,640]{2,1,0:T(8,128)S(1)} %collective-permute-done.7.rows_a, f32[2,64,640]{2,1,0:T(8,128)S(1)} %collective-permute-done.8.rows_b, ...), custom_call_target="tpu_custom_call", output_to_operand_aliasing={{}: (1, {})} | custom-call | tf_op jit(solution)/shard_map/pallas_call | solution.py:490
  121.1 0.0 collective-permute-done.13
  121.1 0.8 fusion
  (3 shorter events, 0.0 us)
Async XLA Ops:
  1.7 18.0 %collective-permute-start = (f32[2,64,512]{2,1,0:T(8,128)S(1)}, f32[2,64,512]{2,1,0:T(8,128)S(1)}, u32[]{:S(2)}, u32[]{:S(2)}) collective-permute-start(f32[2,64,512]{2,1,0:T(8,128)S(1)} %get-tuple-element.55), channel_id=1, source_target_pairs={{0,16},{32,48},{64,80},{96,112},{128,144},{160,176},{192,208},{224... | collective-permute-start | bytes 786440 | tf_op jit(solution)/shard_map/ppermute | solution.py:503
  2.4 17.4 %collective-permute-start.1 = (f32[2,64,512]{2,1,0:T(8,128)S(1)}, f32[2,64,512]{2,1,0:T(8,128)S(1)}, u32[]{:S(2)}, u32[]{:S(2)}) collective-permute-start(f32[2,64,512]{2,1,0:T(8,128)S(1)} %get-tuple-element.54), channel_id=1, source_target_pairs={{16,32},{48,64},{80,96},{112,128},{144,160},{176,192},{208,224},{3... | collective-permute-start | bytes 786440 | tf_op jit(solution)/shard_map/ppermute | solution.py:503
  7.9 1.6 %copy-start = (f32[2,512,512]{2,1,0:T(8,128)S(1)}, f32[2,512,512]{2,1,0:T(8,128)}, u32[]{:S(2)}) copy-start(f32[2,512,512]{2,1,0:T(8,128)} %tile.5) | copy-start | bytes 6291460
  9.5 10.2 %copy-start.3 = (s32[2]{0:T(128)}, s32[2]{0:T(128)S(1)}, u32[]{:S(2)}) copy-start(s32[2]{0:T(128)S(1)} %pad_add_fusion.sides) | copy-start | bytes 28
  10.5 21.6 %collective-permute-start.2 = (f32[512,128]{1,0:T(8,128)S(1)}, f32[512,128]{1,0:T(8,128)S(1)}, u32[]{:S(2)}, u32[]{:S(2)}) collective-permute-start(f32[512,128]{1,0:T(8,128)S(1)} %get-tuple-element.32), channel_id=1, source_target_pairs={{0,1},{2,3},{4,5},{6,7},{8,9},{10,11},{12,13},{14,15},{1,0},{3,2},... | collective-permute-start | bytes 786440 | tf_op jit(solution)/shard_map/ppermute | solution.py:503
  11.8 20.3 %collective-permute-start.3 = (f32[512,128]{1,0:T(8,128)S(1)}, f32[512,128]{1,0:T(8,128)}, u32[]{:S(2)}, u32[]{:S(2)}) collective-permute-start(f32[512,128]{1,0:T(8,128)S(1)} %get-tuple-element.33), channel_id=1, source_target_pairs={{1,2},{3,4},{5,6},{7,8},{9,10},{11,12},{13,14},{2,1},{4,3},{6,5},{... | collective-permute-start | bytes 786440 | tf_op jit(solution)/shard_map/ppermute | solution.py:503
  19.7 16.2 %copy-start.1 = (f32[2,64,512]{2,1,0:T(8,128)}, f32[2,64,512]{2,1,0:T(8,128)S(1)}, u32[]{:S(2)}) copy-start(f32[2,64,512]{2,1,0:T(8,128)S(1)} %collective-permute-done.rows_a) | copy-start | bytes 786436
  19.8 16.2 %copy-start.2 = (f32[2,64,512]{2,1,0:T(8,128)}, f32[2,64,512]{2,1,0:T(8,128)S(1)}, u32[]{:S(2)}) copy-start(f32[2,64,512]{2,1,0:T(8,128)S(1)} %collective-permute-done.1.rows_b) | copy-start | bytes 786436
  20.6 11.5 %collective-permute-start.4 = (f32[128,128]{1,0:T(8,128)S(1)}, f32[128,128]{1,0:T(8,128)S(1)}, u32[]{:S(2)}, u32[]{:S(2)}) collective-permute-start(f32[128,128]{1,0:T(8,128)S(1)} %get-tuple-element.34), channel_id=1, source_target_pairs={{0,1},{2,3},{4,5},{6,7},{8,9},{10,11},{12,13},{14,15},{1,0},{3,2},... | collective-permute-start | bytes 196616 | tf_op jit(solution)/shard_map/ppermute | solution.py:503
  30.1 5.9 %collective-permute-start.5 = (f32[128,128]{1,0:T(8,128)S(1)}, f32[128,128]{1,0:T(8,128)S(1)}, u32[]{:S(2)}, u32[]{:S(2)}) collective-permute-start(f32[128,128]{1,0:T(8,128)S(1)} %get-tuple-element.35), channel_id=1, source_target_pairs={{1,2},{3,4},{5,6},{7,8},{9,10},{11,12},{13,14},{2,1},{4,3},{6,5},{... | collective-permute-start | bytes 196616 | tf_op jit(solution)/shard_map/ppermute | solution.py:503
  32.0 3.9 %copy-start.5 = (f32[512,128]{1,0:T(8,128)}, f32[512,128]{1,0:T(8,128)S(1)}, u32[]{:S(2)}) copy-start(f32[512,128]{1,0:T(8,128)S(1)} %collective-permute-done.2.cols_a) | copy-start | bytes 786436
  32.0 3.9 %copy-start.6 = (f32[128,128]{1,0:T(8,128)}, f32[128,128]{1,0:T(8,128)S(1)}, u32[]{:S(2)}) copy-start(f32[128,128]{1,0:T(8,128)S(1)} %collective-permute-done.4.corners_a) | copy-start | bytes 196612
  36.0 0.6 copy-start.7
  46.0 1.9 %collective-permute-start.6 = (f32[512,128]{1,0:T(8,128)S(1)}, f32[512,128]{1,0:T(8,128)S(1)}, u32[]{:S(2)}, u32[]{:S(2)}) collective-permute-start(f32[512,128]{1,0:T(8,128)S(1)} %constant_dynamic-slice_fusion), channel_id=1, source_target_pairs={{0,1},{1,0},{2,3},{3,2},{4,5},{5,4},{6,7},{7,6},{8,9},{9,8},{10,11... | collective-permute-start | bytes 786440 | tf_op jit(solution)/shard_map/ppermute | solution.py:503
  49.7 33.9 %all-to-all-start = ((f32[16,32,128]{2,1,0:T(8,128)}), f32[16,32,128]{2,1,0:T(8,128)S(1)}, u32[]{:S(2)}, u32[]{:S(2)}) async-start(f32[16,32,128]{2,1,0:T(8,128)} %bitcast.5), calls=%async_computation | async-start | bytes 524288 | tf_op jit(solution)/shard_map/all_to_all | solution.py:519
  56.4 50.2 %copy-start.4 = (s32[2]{0:T(128)S(1)}, s32[2]{0:T(128)}, u32[]{:S(2)}) copy-start(s32[2]{0:T(128)} %copy-done.3) | copy-start | bytes 28
  61.1 39.1 %collective-permute-start.7 = (f32[2,64,640]{2,1,0:T(8,128)}, f32[2,64,640]{2,1,0:T(8,128)S(1)}, u32[]{:S(2)}, u32[]{:S(2)}) collective-permute-start(f32[2,64,640]{2,1,0:T(8,128)} %get-tuple-element.40), channel_id=1, source_target_pairs={{0,16},{32,48},{64,80},{96,112},{128,144},{160,176},{192,208},{224... | collective-permute-start | bytes 983048 | tf_op jit(solution)/shard_map/ppermute | solution.py:503
  62.4 37.8 %collective-permute-start.8 = (f32[2,64,640]{2,1,0:T(8,128)}, f32[2,64,640]{2,1,0:T(8,128)S(1)}, u32[]{:S(2)}, u32[]{:S(2)}) collective-permute-start(f32[2,64,640]{2,1,0:T(8,128)} %get-tuple-element.41), channel_id=1, source_target_pairs={{16,32},{48,64},{80,96},{112,128},{144,160},{176,192},{208,224},{3... | collective-permute-start | bytes 983048 | tf_op jit(solution)/shard_map/ppermute | solution.py:503
  78.1 22.0 %collective-permute-start.10 = (f32[512,128]{1,0:T(8,128)}, f32[512,128]{1,0:T(8,128)S(1)}, u32[]{:S(2)}, u32[]{:S(2)}) collective-permute-start(f32[512,128]{1,0:T(8,128)} %get-tuple-element.43), channel_id=1, source_target_pairs={{1,2},{3,4},{5,6},{7,8},{9,10},{11,12},{13,14},{2,1},{4,3},{6,5},{... | collective-permute-start | bytes 786440 | tf_op jit(solution)/shard_map/ppermute | solution.py:503
  83.5 16.7 %collective-permute-start.9 = (f32[512,128]{1,0:T(8,128)}, f32[512,128]{1,0:T(8,128)S(1)}, u32[]{:S(2)}, u32[]{:S(2)}) collective-permute-start(f32[512,128]{1,0:T(8,128)} %get-tuple-element.42), channel_id=1, source_target_pairs={{0,1},{2,3},{4,5},{6,7},{8,9},{10,11},{12,13},{14,15},{1,0},{3,2},... | collective-permute-start | bytes 786440 | tf_op jit(solution)/shard_map/ppermute | solution.py:503
  100.9 16.7 %all-to-all-start.2 = ((f32[16,32,128]{2,1,0:T(8,128)}), f32[16,32,128]{2,1,0:T(8,128)S(1)}, u32[]{:S(2)}, u32[]{:S(2)}) async-start(f32[16,32,128]{2,1,0:T(8,128)} %broadcast_in_dim.5), calls=%async_computation.2 | async-start | bytes 524288 | tf_op jit(solution)/shard_map/all_to_all | solution.py:524
  107.3 7.4 %collective-permute-start.11 = (f32[128,128]{1,0:T(8,128)S(1)}, f32[128,128]{1,0:T(8,128)S(1)}, u32[]{:S(2)}, u32[]{:S(2)}) collective-permute-start(f32[128,128]{1,0:T(8,128)S(1)} %get-tuple-element.49), channel_id=1, source_target_pairs={{0,1},{2,3},{4,5},{6,7},{8,9},{10,11},{12,13},{14,15},{1,0},{3,2},... | collective-permute-start | bytes 196616 | tf_op jit(solution)/shard_map/ppermute | solution.py:503
  110.8 6.8 %collective-permute-start.12 = (f32[128,128]{1,0:T(8,128)S(1)}, f32[128,128]{1,0:T(8,128)S(1)}, u32[]{:S(2)}, u32[]{:S(2)}) collective-permute-start(f32[128,128]{1,0:T(8,128)S(1)} %get-tuple-element.50), channel_id=1, source_target_pairs={{1,2},{3,4},{5,6},{7,8},{9,10},{11,12},{13,14},{2,1},{4,3},{6,5},{... | collective-permute-start | bytes 196616 | tf_op jit(solution)/shard_map/ppermute | solution.py:503
  117.6 3.5 %collective-permute-start.13 = (f32[512,128]{1,0:T(8,128)S(1)}, f32[512,128]{1,0:T(8,128)S(1)}, u32[]{:S(2)}, u32[]{:S(2)}) collective-permute-start(f32[512,128]{1,0:T(8,128)S(1)} %bitcast.10), channel_id=1, source_target_pairs={{0,1},{1,0},{2,3},{3,2},{4,5},{5,4},{6,7},{7,6},{8,9},{9,8},{10,11... | collective-permute-start | bytes 786440 | tf_op jit(solution)/shard_map/ppermute | solution.py:503

commit v3 on v2

--- a/solution.py
+++ b/solution.py
@@ -215,7 +215,7 @@
 
 def late_kernel(
     counts, offsets, sides, tile, rows_a, rows_b, amps, probe, forward, inverse, cols_a, cols_b, corners_a, corners_b,
-    probe_before, patch_grads, probe_total, *scratch
+    probe_before, patch_grads, probe_kept, probe_sent, probe_total, *scratch
 ):
     extended, side_sem, sem = scratch[0], scratch[-3], scratch[-2]
     scratch = scratch[:-3] + scratch[-2:]
@@ -270,6 +270,8 @@
     run_slots(
         False, counts, offsets, amps, patch_grads, probe, probe_total, scratch, copies, strip_copies(rows_a, rows_b)
     )
+    half = MODES // 2
+    put_by_side(even_col, probe_kept, probe_sent, probe_total[:half], probe_total[half:])
 
 
 def put_by_side(even, a, b, after, before):
@@ -328,7 +330,7 @@
 
 
 def deposit_kernel(
-    counts, offsets, sides, early_grads, late_grads, inner, rows_a, rows_b, cols_a, cols_b, total, held, flank, sems, out_sem
+    counts, offsets, sides, early_grads, late_grads, inner, top, bottom, cols_a, cols_b, total, held, sems, out_sem
 ):
     n = PATCH
     live, first = early_slots(counts, offsets)
@@ -379,67 +381,49 @@
     def _():
         add(live - 1, turned(live - 1))
 
+    copies = []
+    for start, rows, out in ((0, HALF, top), (HALF, TILE, inner), (HALF + TILE, HALF, bottom)):
+        for b in range(TILE // n):
+            near, far = total.at[:, b + 1, pl.ds(start, rows), :], out.at[:, :, pl.ds(b * n, n)]
+            copies.append(pltpu.make_async_copy(near, far, out_sem))
+    for c in copies:
+        c.start()
     low = lane_iota(EXT) < HALF
-    for p in range(2):
-        flank[p] = pltpu.roll(jnp.where(low, total[p, BLOCKS - 1], total[p, 0]), HALF, 1)
-
-    def copies(above, below):
-        made = []
-        for start, rows, out in ((0, HALF, above), (HALF, TILE, inner), (HALF + TILE, HALF, below)):
-            for b in range(TILE // n):
-                made.append((total.at[:, b + 1, pl.ds(start, rows), :], out.at[:, :, pl.ds(b * n, n)]))
-        made.append((flank.at[:, pl.ds(0, HALF), :], above.at[:, :, pl.ds(TILE, n)]))
-        made.append((flank.at[:, pl.ds(HALF + TILE, HALF), :], below.at[:, :, pl.ds(TILE, n)]))
-        return [pltpu.make_async_copy(near, far, out_sem) for near, far in made]
-
-    def start(above, below):
-        for c in copies(above, below):
-            c.start()
-
-    @pl.when(sides[0] == 0)
-    def _():
-        start(rows_b, rows_a)
-
-    @pl.when(sides[0] != 0)
-    def _():
-        start(rows_a, rows_b)
-
-    low = lane_iota(TILE) < HALF
-    own = flank[0, HALF : HALF + TILE, :], flank[1, HALF : HALF + TILE, :]
     put_by_side(
         sides[1] == 0,
         cols_a,
         cols_b,
-        jnp.where(low, pltpu.roll(own[0], HALF, 1), own[1]),
-        jnp.where(low, own[0], pltpu.roll(own[1], HALF, 1)),
-    )
-    for c in copies(rows_a, rows_b):
+        jnp.where(low, total[0, BLOCKS - 1], pltpu.roll(total[1, BLOCKS - 1], HALF, 1)),
+        jnp.where(low, pltpu.roll(total[0, 0], HALF, 1), total[1, 0]),
+    )
+    for c in copies:
         c.wait()
 
 
-def corner_kernel(sides, rows_a, rows_b, corners_a, corners_b, held, sem):
-    even_row = sides[0] == 0
-    copies = [pltpu.make_async_copy(r.at[:, :, pl.ds(TILE, PATCH)], held.at[i], sem) for i, r in enumerate((rows_a, rows_b))]
-    for c in copies:
-        c.start()
-    for c in copies:
-        c.wait()
-    low = lane_iota(HALF) < HALF
-    a, b = held[0], held[1]
-    for i, part in enumerate((jnp.where(even_row, b, a), jnp.where(even_row, a, b))):
-        rows = pl.ds(i * HALF, HALF)
-        put_by_side(
-            sides[1] == 0,
-            corners_a.at[rows, :],
-            corners_b.at[rows, :],
-            jnp.where(low, pltpu.roll(part[0], HALF, 1), part[1]),
-            jnp.where(low, part[0], pltpu.roll(part[1], HALF, 1)),
+def side_terms(even_col, a, b):
+    low = lane_iota(a.shape[0]) < HALF
+    from_left, from_right = jnp.where(even_col, b, a), jnp.where(even_col, a, b)
+    first = (jnp.where(low, from_left, 0.0), jnp.where(low, pltpu.roll(from_left, HALF, 1), 0.0))
+    last = (jnp.where(low, 0.0, pltpu.roll(from_right, HALF, 1)), jnp.where(low, 0.0, from_right))
+    return first, last
+
+
+def edges_kernel(sides, top, bottom, cols_a, cols_b, rows_a, rows_b):
+    end = TILE - PATCH
+    sent = []
+    for part, rows in ((top, slice(0, HALF)), (bottom, slice(HALF + TILE, EXT))):
+        first, last = side_terms(sides[1] == 0, cols_a[rows, :], cols_b[rows, :])
+        sent.append(
+            [
+                jnp.concatenate([part[p, :, :PATCH] + first[p], part[p, :, PATCH:end], part[p, :, end:] + last[p]], 1)
+                for p in range(2)
+            ]
         )
-
-
-def merge_kernel(
-    sides, inner, rows_a, rows_b, cols_a, cols_b, corners_a, corners_b, out, left, right, top, bottom, strips, sems, sem
-):
+    for p in range(2):
+        put_by_side(sides[0] == 0, rows_a.at[p], rows_b.at[p], sent[1][p], sent[0][p])
+
+
+def merge_kernel(sides, inner, cols_a, cols_b, rows_a, rows_b, out, left, right, top, bottom, sems):
     end = TILE - PATCH
     regions = (
         (out.at[:, :, pl.ds(0, PATCH)], left),
@@ -448,30 +432,20 @@
         (out.at[:, pl.ds(TILE - HALF, HALF), pl.ds(PATCH, TILE - 2 * PATCH)], bottom),
     )
     loads = [pltpu.make_async_copy(far, near, sems.at[i]) for i, (far, near) in enumerate(regions)]
-    loads += [pltpu.make_async_copy(r.at[:, :, pl.ds(0, TILE)], strips.at[i], sem) for i, r in enumerate((rows_a, rows_b))]
     for c in loads:
         c.start()
-    even_row, even_col = sides[0] == 0, sides[1] == 0
-
-    def both_sides(a, b):
-        low = lane_iota(a.shape[0]) < HALF
-        from_left, from_right = jnp.where(even_col, b, a), jnp.where(even_col, a, b)
-        first = (jnp.where(low, from_left, 0.0), jnp.where(low, pltpu.roll(from_left, HALF, 1), 0.0))
-        last = (jnp.where(low, 0.0, pltpu.roll(from_right, HALF, 1)), jnp.where(low, 0.0, from_right))
-        return first, last
-
-    sides_terms = both_sides(cols_a[...], cols_b[...])
-    corner_terms = both_sides(corners_a[...], corners_b[...])
+    a, b = rows_a[...], rows_b[...]
+    above, below = jnp.where(sides[0] == 0, b, a), jnp.where(sides[0] == 0, a, b)
+    own = slice(HALF, HALF + TILE)
+    terms = side_terms(sides[1] == 0, cols_a[own, :], cols_b[own, :])
     for c in loads:
         c.wait()
-    a, b = strips[0], strips[1]
-    above, below = jnp.where(even_row, b, a), jnp.where(even_row, a, b)
     middle = slice(PATCH, end)
     for p in range(2):
-        for i, (near, lanes) in enumerate(((left, slice(0, PATCH)), (right, slice(end, TILE)))):
-            near[p] += sides_terms[i][p]
-            near[p, :HALF, :] += above[p, :, lanes] + corner_terms[i][p][:HALF]
-            near[p, TILE - HALF :, :] += below[p, :, lanes] + corner_terms[i][p][HALF:]
+        for near, term, lanes in ((left, terms[0][p], slice(0, PATCH)), (right, terms[1][p], slice(end, TILE))):
+            near[p] += term
+            near[p, :HALF, :] += above[p, :, lanes]
+            near[p, TILE - HALF :, :] += below[p, :, lanes]
         top[p] += above[p, :, middle]
         bottom[p] += below[p, :, middle]
     stores = [pltpu.make_async_copy(near, far, sems.at[i]) for i, (far, near) in enumerate(regions)]
@@ -501,12 +475,6 @@
 def swap(value, axes, size, first):
     pairs = [(i, i + 1) for i in range(first, size - 1, 2)]
     return lax.ppermute(value, axes, pairs + [(j, i) for i, j in pairs])
-
-
-def halve(x, axis):
-    half, me = x.shape[0] // 2, lax.axis_index(axis)
-    sent = lax.dynamic_slice_in_dim(x, (1 - me) * half, half, 0)
-    return lax.dynamic_slice_in_dim(x, me * half, half, 0) + swap(sent, axis, 2, 0)
 
 
 def double(x, axis):
@@ -544,7 +512,7 @@
         pltpu.SemaphoreType.DMA((SLOTS,)),
     ]
     grads_shape, probe_shape = (SLOTS, 2, PATCH, PATCH), (MODES, 2, PATCH, PATCH)
-    wide_row, column = (2, HALF, TILE + PATCH), (TILE, PATCH)
+    strip, column = (2, HALF, TILE), (TILE, PATCH)
     block = pltpu.VMEM((2, TILE, PATCH), jnp.float32)
     low, high = 0, TILE - HALF
     after = lax.dynamic_slice_in_dim(tile, jnp.where(odd_row == 0, high, low), HALF, 1)
@@ -568,46 +536,43 @@
     )
     corners_b = swap(corners_b, COL, cols, 1)
     corners_a = swap(corners_a, COL, cols, 0)
-    late_scratch = slot_scratch[:-2] + [pltpu.SemaphoreType.DMA] + slot_scratch[-2:]
-    late_grads, probe_total = call(
-        late_kernel, [SMEM] * 3 + [HBM] * 7 + [VMEM] * 5, [HBM, VMEM], [grads_shape, probe_shape], late_scratch,
+    half_shape = (MODES // 2, 2, PATCH, PATCH)
+    late_scratch = [pltpu.VMEM(probe_shape, jnp.float32)] + slot_scratch[:-2] + [pltpu.SemaphoreType.DMA] + slot_scratch[-2:]
+    late_grads, probe_kept, probe_sent = call(
+        late_kernel, [SMEM] * 3 + [HBM] * 7 + [VMEM] * 5, [HBM, VMEM, VMEM], [grads_shape, half_shape, half_shape], late_scratch,
         counts, offsets, sides, tile, rows_a, rows_b, amps, probe, forward, inverse, cols_a, cols_b, corners_a, corners_b, probe_early
     )
 
-    sums = halve(probe_total.reshape(-1, PATCH), "core")
-    inner, rows_a, rows_b, cols_a, cols_b = call(
+    sums = (probe_kept + swap(probe_sent, "core", 2, 0)).reshape(-1, PATCH)
+    inner, top, bottom, cols_a, cols_b = call(
         deposit_kernel, [SMEM] * 3 + [HBM] * 2, [HBM] * 3 + [VMEM] * 2,
-        [(2, TILE, TILE), wide_row, wide_row, column, column],
+        [(2, TILE, TILE), strip, strip, (EXT, PATCH), (EXT, PATCH)],
         [
             pltpu.VMEM((2, BLOCKS, EXT, PATCH), jnp.float32),
             pltpu.VMEM(grads_shape, jnp.float32),
-            pltpu.VMEM((2, EXT, PATCH), jnp.float32),
             pltpu.SemaphoreType.DMA((SLOTS,)),
             pltpu.SemaphoreType.DMA,
         ],
         counts, offsets, sides, early_grads, late_grads
     )
-    rows_b = swap(rows_b, ROW, rows, 1)
     cols_b = swap(cols_b, COL, cols, 1)
-    rows_a = swap(rows_a, ROW, rows, 0)
     cols_a = swap(cols_a, COL, cols, 0)
     plane, line = ("x", "y"), ("zh", "zl")
     sums = jnp.sum(deal(sums, plane, sizes), 0)
+    rows_a, rows_b = call(
+        edges_kernel, [SMEM] + [VMEM] * 4, [VMEM] * 2, [strip] * 2, [], sides, top, bottom, cols_a, cols_b, limit=16
+    )
     sums = jnp.sum(spread(sums, line, sizes), 0)
-    sums, rows_a, rows_b, cols_a, cols_b = lax.optimization_barrier((sums, rows_a, rows_b, cols_a, cols_b))
-    corners_a, corners_b = call(
-        corner_kernel, [SMEM] + [HBM] * 2, [VMEM] * 2, [(PATCH, PATCH)] * 2, [piece, pltpu.SemaphoreType.DMA],
-        sides, rows_a, rows_b, limit=16
-    )
-    corners_b = swap(corners_b, COL, cols, 1)
-    corners_a = swap(corners_a, COL, cols, 0)
+    sums, rows_a, rows_b = lax.optimization_barrier((sums, rows_a, rows_b))
+    rows_b = swap(rows_b, ROW, rows, 1)
+    rows_a = swap(rows_a, ROW, rows, 0)
     sums = spread(sums, plane, sizes).reshape(-1, PATCH)
-    sums, corners_a, corners_b = lax.optimization_barrier((sums, corners_a, corners_b))
+    sums, rows_a, rows_b = lax.optimization_barrier((sums, rows_a, rows_b))
     end = pltpu.VMEM((2, HALF, TILE - 2 * PATCH), jnp.float32)
     (object_grad,) = call(
-        merge_kernel, [SMEM] + [HBM] * 3 + [VMEM] * 4, [HBM], [(2, TILE, TILE)],
-        [block, block, end, end, pltpu.VMEM((2, 2, HALF, TILE), jnp.float32), pltpu.SemaphoreType.DMA((4,)), pltpu.SemaphoreType.DMA],
-        sides, inner, rows_a, rows_b, cols_a, cols_b, corners_a, corners_b, aliases={1: 0}, limit=16
+        merge_kernel, [SMEM, HBM] + [VMEM] * 4, [HBM], [(2, TILE, TILE)],
+        [block, block, end, end, pltpu.SemaphoreType.DMA((4,))],
+        sides, inner, cols_a, cols_b, rows_a, rows_b, aliases={1: 0}, limit=16
     )
     factor = 1.0 / math.sqrt(rows * cols * SLOTS)
     probe_grad = (double(sums, "core") * factor).reshape(probe_shape)

time: 124 us -> 119 us (0.960)
  starting transfers between devices: 65.7 us -> 52.3 us
  waiting for transfers between devices: 7.98 us -> 14.9 us
  Pallas kernels: 22.5 us -> 28.8 us
  blocking collectives: 16.5 us -> 12 us
    ppermute x14 -> x12, starting transfers between devices: 53.4 us -> 29 us  [swap(): return lax.ppermute(value, axes, pairs + [(j, i) for i, j in pairs])]
    all_to_all x1, starting transfers between devices: 6.71 us -> 14.6 us  [deal(): return lax.all_to_all(x.reshape(count, -1, PATCH), axes, 0, 0, tiled=True)]
    pallas_call x7, Pallas kernels: 22.5 us -> 28.8 us  [call(): pl.pallas_call(kernel, in_specs=in_specs, out_specs=out_specs, out_shape=...]
    all_to_all x1, waiting for transfers between devices: 0.01 us -> 5.33 us  [spread(): lax.all_to_all(jnp.broadcast_to(x[None], (count, *x.shape)), axes, 0, 0,...]
    all_to_all x1, blocking collectives: 16.5 us -> 12 us  [spread(): lax.all_to_all(jnp.broadcast_to(x[None], (count, *x.shape)), axes, 0, 0,...]
    all_to_all x1, starting transfers between devices: 5.64 us -> 8.67 us  [spread(): lax.all_to_all(jnp.broadcast_to(x[None], (count, *x.shape)), axes, 0, 0,...]
    unnamed x16 -> x20, local copies, waits for them, and re-layouts: 2.23 us -> 4.13 us
    ppermute x14 -> x12, waiting for transfers between devices: 7.98 us -> 9.56 us  [swap(): return lax.ppermute(value, axes, pairs + [(j, i) for i, j in pairs])]
  transfers between devices with their start and end apart: 16 -> 14, of which waited for: 3 -> 5; matrix products, arithmetic and copies ran while one was open for 0% -> 1% of each run, Pallas kernels for 11% -> 17%
where the time goes in v3:
time: 119 us; the launch traced here: 118 us
  starting transfers between devices  52.3 us (44%)
  Pallas kernels  28.8 us (24%)
  waiting for transfers between devices  14.9 us (13%)
  blocking collectives  12 us (10%)
  local copies, waits for them, and re-layouts  5.88 us (5%)
  other arithmetic  2.67 us (2%)
  between operations  1.58 us (1%)
    ppermute x12, starting transfers between devices, swap(): return lax.ppermute(value, axes, pairs + [(j, i) for i, j in pairs])  29 us
    pallas_call x7, Pallas kernels, call(): pl.pallas_call(kernel, in_specs=in_specs, out_specs=out_specs, out_shape=...  28.8 us
    all_to_all x1, starting transfers between devices, deal(): return lax.all_to_all(x.reshape(count, -1, PATCH), axes, 0, 0, tiled=True)  14.6 us
    all_to_all x1, blocking collectives, spread(): lax.all_to_all(jnp.broadcast_to(x[None], (count, *x.shape)), axes, 0, 0,...  12 us
    ppermute x12, waiting for transfers between devices, swap(): return lax.ppermute(value, axes, pairs + [(j, i) for i, j in pairs])  9.56 us
    all_to_all x1, starting transfers between devices, spread(): lax.all_to_all(jnp.broadcast_to(x[None], (count, *x.shape)), axes, 0, 0,...  8.67 us
    all_to_all x1, waiting for transfers between devices, spread(): lax.all_to_all(jnp.broadcast_to(x[None], (count, *x.shape)), axes, 0, 0,...  5.33 us
    unnamed x20, local copies, waits for them, and re-layouts  4.13 us
  transfers between devices with their start and end apart: 14, of which 5 were waited for; matrix products, arithmetic and copies ran while one was open for 1% of the time, Pallas kernels for 17%

profile of v3, /device:TPU:15, one launch (start us, length us, event | category | flops | bytes accessed | tf_op | source)
XLA Modules:
  0.0 118.1 jit_solution(14975110894149385619)
XLA Ops:
  0.6 1.1 constant_dynamic-slice_fusion
  1.7 4.8 %collective-permute-start.1 = (f32[2,64,512]{2,1,0:T(8,128)S(1)}, f32[2,64,512]{2,1,0:T(8,128)S(1)}, u32[]{:S(2)}, u32[]{:S(2)}) collective-permute-start(f32[2,64,512]{2,1,0:T(8,128)S(1)} %get-tuple-element.52), channel_id=1, source_target_pairs={{16,32},{48,64},{80,96},{112,128},{144,160},{176,192},{208,224},{3... | collective-permute-start | bytes 786440 | tf_op jit(solution)/shard_map/ppermute | solution.py:477
  6.5 0.1 collective-permute-start
  6.7 0.1 pad_add_fusion.sides
  6.7 0.0 copy-start
  6.7 1.6 %copy-done = f32[2,512,512]{2,1,0:T(8,128)S(1)} copy-done((f32[2,512,512]{2,1,0:T(8,128)S(1)}, f32[2,512,512]{2,1,0:T(8,128)}, u32[]{:S(2)}) %copy-start) | copy-done | bytes 2097176
  8.3 0.0 copy-start.5
  8.3 0.9 shard_map.87
  9.3 1.0 collective-permute-start.2
  10.3 3.4 %collective-permute-start.3 = (f32[512,128]{1,0:T(8,128)S(1)}, f32[512,128]{1,0:T(8,128)}, u32[]{:S(2)}, u32[]{:S(2)}) collective-permute-start(f32[512,128]{1,0:T(8,128)S(1)} %get-tuple-element.32), channel_id=1, source_target_pairs={{1,2},{3,4},{5,6},{7,8},{9,10},{11,12},{13,14},{2,1},{4,3},{6,5},{... | collective-permute-start | bytes 786440 | tf_op jit(solution)/shard_map/ppermute | solution.py:477
  14.4 10.0 %shard_map.86 = (f32[16,2,128,128]{3,2,1,0:T(8,128)}, f32[4,2,128,128]{3,2,1,0:T(8,128)}) custom-call(s32[1,1]{1,0:T(1,128)S(6)} %copy.11.counts, s32[1,1,2,16]{3,2,1,0:T(2,128)} %bitcast.12, f32[2,512,512]{2,1,0:T(8,128)} %tile.5, f32[16,128,128]{2,1,0:T(8,128)} %bitcast.7, f32[4,2,128,128]{3,2,1,0:T(8,128)} %probe.3, ...), custom_call_target="tpu_custom_call" | custom-call | tf_op jit(solution)/shard_map/pallas_call | solution.py:464
  24.4 0.0 collective-permute-done.1.rows_b
  24.4 0.0 copy-start.1
  24.5 0.0 collective-permute-done.rows_a
  24.5 0.0 copy-start.2
  24.5 0.0 copy-done.5
  24.5 0.8 shard_map.88
  25.3 0.1 collective-permute-start.4
  25.4 2.1 %collective-permute-start.5 = (f32[128,128]{1,0:T(8,128)S(1)}, f32[128,128]{1,0:T(8,128)S(1)}, u32[]{:S(2)}, u32[]{:S(2)}) collective-permute-start(f32[128,128]{1,0:T(8,128)S(1)} %get-tuple-element.34), channel_id=1, source_target_pairs={{1,2},{3,4},{5,6},{7,8},{9,10},{11,12},{13,14},{2,1},{4,3},{6,5},{... | collective-permute-start | bytes 196616 | tf_op jit(solution)/shard_map/ppermute | solution.py:477
  27.5 0.0 collective-permute-done.2.cols_a
  27.5 0.0 copy-start.7
  27.5 0.0 collective-permute-done.3.cols_b
  27.5 0.0 collective-permute-done.4.corners_a
  27.5 0.0 copy-start.8
  27.5 3.4 %collective-permute-done.5.corners_b = f32[128,128]{1,0:T(8,128)S(1)} collective-permute-done((f32[128,128]{1,0:T(8,128)S(1)}, f32[128,128]{1,0:T(8,128)S(1)}, u32[]{:S(2)}, u32[]{:S(2)}) %collective-permute-start.5) | collective-permute-done | bytes 65568 | tf_op jit(solution)/shard_map/ppermute | solution.py:477
  31.0 0.0 copy-done.1
  31.0 0.0 copy-done.2
  31.0 0.0 copy-done.7
  31.0 0.0 copy-done.8
  31.0 0.0 copy-start.9
  31.0 0.6 copy-done.9
  31.6 8.5 %shard_map.89 = (f32[16,2,128,128]{3,2,1,0:T(8,128)}, f32[2,2,128,128]{3,2,1,0:T(8,128)}, f32[2,2,128,128]{3,2,1,0:T(8,128)}) custom-call(s32[1,1]{1,0:T(1,128)S(6)} %copy.11.counts, s32[1,1,2,16]{3,2,1,0:T(2,128)} %bitcast.13, s32[2]{0:T(128)} %copy-done.5, f32[2,512,512]{2,1,0:T(8,128)} %tile.5, f32[2,64,512]{2,1,0:T(8,128)} %copy-done.2, ...), custom_call_target="tpu_custom_call" | custom-call | tf_op jit(solution)/shard_map/pallas_call | solution.py:464
  40.1 7.8 %collective-permute-start.8 = (f32[2,2,128,128]{3,2,1,0:T(8,128)}, f32[2,2,128,128]{3,2,1,0:T(8,128)S(1)}, u32[]{:S(2)}, u32[]{:S(2)}) collective-permute-start(f32[2,2,128,128]{3,2,1,0:T(8,128)} %get-tuple-element.41), channel_id=1, source_target_pairs={{0,1},{1,0},{2,3},{3,2},{4,5},{5,4},{6,7},{7,6},{8,9},{9,8},{10,11... | collective-permute-start | bytes 786440 | tf_op jit(solution)/shard_map/ppermute | solution.py:477
  48.0 1.4 %collective-permute-done.8 = f32[2,2,128,128]{3,2,1,0:T(8,128)S(1)} collective-permute-done((f32[2,2,128,128]{3,2,1,0:T(8,128)}, f32[2,2,128,128]{3,2,1,0:T(8,128)S(1)}, u32[]{:S(2)}, u32[]{:S(2)}) %collective-permute-start.8) | collective-permute-done | bytes 262176 | tf_op jit(solution)/shard_map/ppermute | solution.py:477
  49.3 1.7 %add.26 = f32[2,2,128,128]{3,2,1,0:T(8,128)} add(f32[2,2,128,128]{3,2,1,0:T(8,128)} %get-tuple-element.40, f32[2,2,128,128]{3,2,1,0:T(8,128)S(1)} %collective-permute-done.8) | non-fusion elementwise | flops 65536 | bytes 786432 | tf_op jit(solution)/shard_map/add | solution.py:546
  51.1 14.6 %all-to-all-start = ((f32[16,32,128]{2,1,0:T(8,128)}), f32[16,32,128]{2,1,0:T(8,128)S(1)}, u32[]{:S(2)}, u32[]{:S(2)}) async-start(f32[16,32,128]{2,1,0:T(8,128)} %bitcast.4), calls=%async_computation | async-start | bytes 524288 | tf_op jit(solution)/shard_map/all_to_all | solution.py:487
  65.6 0.0 copy-start.6
  65.6 4.8 %shard_map.90 = (f32[2,512,512]{2,1,0:T(8,128)}, f32[2,64,512]{2,1,0:T(8,128)}, f32[2,64,512]{2,1,0:T(8,128)}, f32[640,128]{1,0:T(8,128)}, f32[640,128]{1,0:T(8,128)}) custom-call(s32[1,1]{1,0:T(1,128)S(6)} %copy.11.counts, s32[1,1,2,16]{3,2,1,0:T(2,128)} %bitcast.14, s32[2]{0:T(128)} %copy-done.5, f32[16,2,128,128]{3,2,1,0:T(8,128)} %get-tuple-element.27.early_grads, ...), custom_call_target="tpu_custom_call" | custom-call | tf_op jit(solution)/shard_map/pallas_call | solution.py:464
  70.5 1.0 collective-permute-start.6
  71.5 1.9 %collective-permute-start.7 = (f32[640,128]{1,0:T(8,128)}, f32[640,128]{1,0:T(8,128)S(1)}, u32[]{:S(2)}, u32[]{:S(2)}) collective-permute-start(f32[640,128]{1,0:T(8,128)} %get-tuple-element.39), channel_id=1, source_target_pairs={{1,2},{3,4},{5,6},{7,8},{9,10},{11,12},{13,14},{2,1},{4,3},{6,5},{... | collective-permute-start | bytes 983048 | tf_op jit(solution)/shard_map/ppermute | solution.py:477
  73.4 0.0 all-to-all-done
  73.5 0.7 broadcast_in_dim.4
  74.1 8.7 %all-to-all-start.1 = ((f32[8,32,128]{2,1,0:T(8,128)}), f32[8,32,128]{2,1,0:T(8,128)S(1)}, u32[]{:S(2)}, u32[]{:S(2)}) async-start(f32[8,32,128]{2,1,0:T(8,128)} %broadcast_in_dim.4), calls=%async_computation.1 | async-start | bytes 262144 | tf_op jit(solution)/shard_map/all_to_all | solution.py:492
  82.8 0.0 collective-permute-done.6.cols_a
  82.8 1.0 collective-permute-done.7.cols_b
  83.8 0.0 copy-done.6
  83.8 0.0 copy-start.3
  83.8 0.9 copy-done.3
  84.7 0.0 copy-start.4
  84.8 0.9 copy-done.4
  85.7 0.7 shard_map.91
  86.4 5.3 %all-to-all-done.1 = f32[8,32,128]{2,1,0:T(8,128)S(1)} async-done(((f32[8,32,128]{2,1,0:T(8,128)}), f32[8,32,128]{2,1,0:T(8,128)S(1)}, u32[]{:S(2)}, u32[]{:S(2)}) %all-to-all-start.1) | async-done | bytes 131104 | tf_op jit(solution)/shard_map/all_to_all | solution.py:492
  91.7 0.3 collective-permute-start.9
  92.0 3.6 %collective-permute-start.10 = (f32[2,64,512]{2,1,0:T(8,128)S(1)}, f32[2,64,512]{2,1,0:T(8,128)S(1)}, u32[]{:S(2)}, u32[]{:S(2)}) collective-permute-start(f32[2,64,512]{2,1,0:T(8,128)S(1)} %get-tuple-element.48), channel_id=1, source_target_pairs={{16,32},{48,64},{80,96},{112,128},{144,160},{176,192},{208,224},{3... | collective-permute-start | bytes 786440 | tf_op jit(solution)/shard_map/ppermute | solution.py:477
  95.6 12.0 %all_to_all.15 = f32[16,32,128]{2,1,0:T(8,128)S(1)} all-to-all(f32[16,32,128]{2,1,0:T(8,128)S(1)} %broadcast_in_dim.5), channel_id=1, replica_groups=mesh['zh'=4,'x'=4,'y'=4,'zl'=2,'core'=2] {'x','y'}, dimensions={0} | all-to-all | bytes 524288 | tf_op jit(solution)/shard_map/all_to_all | solution.py:492
  107.7 0.0 collective-permute-done.9.rows_a
  107.7 3.7 %collective-permute-done.10.rows_b = f32[2,64,512]{2,1,0:T(8,128)S(1)} collective-permute-done((f32[2,64,512]{2,1,0:T(8,128)S(1)}, f32[2,64,512]{2,1,0:T(8,128)S(1)}, u32[]{:S(2)}, u32[]{:S(2)}) %collective-permute-start.10) | collective-permute-done | bytes 262176 | tf_op jit(solution)/shard_map/ppermute | solution.py:477
  111.4 2.8 %collective-permute-start.11 = (f32[512,128]{1,0:T(8,128)S(1)}, f32[512,128]{1,0:T(8,128)S(1)}, u32[]{:S(2)}, u32[]{:S(2)}) collective-permute-start(f32[512,128]{1,0:T(8,128)S(1)} %bitcast.9), channel_id=1, source_target_pairs={{0,1},{1,0},{2,3},{3,2},{4,5},{5,4},{6,7},{7,6},{8,9},{9,8},{10,11... | collective-permute-start | bytes 786440 | tf_op jit(solution)/shard_map/ppermute | solution.py:477
  114.2 3.0 %shard_map.92 = f32[2,512,512]{2,1,0:T(8,128)} custom-call(s32[2]{0:T(128)S(1)} %copy-done.6, f32[2,512,512]{2,1,0:T(8,128)} %get-tuple-element.37.inner, f32[640,128]{1,0:T(8,128)S(1)} %collective-permute-done.6.cols_a, f32[640,128]{1,0:T(8,128)S(1)} %collective-permute-done.7.cols_b, ...), custom_call_target="tpu_custom_call", output_to_operand_aliasing={{}: (1, {})} | custom-call | tf_op jit(solution)/shard_map/pallas_call | solution.py:464
  117.2 0.0 collective-permute-done.11
  117.2 0.9 fusion
  (3 shorter events, 0.1 us)
Async XLA Ops:
  1.7 22.7 %collective-permute-start.1 = (f32[2,64,512]{2,1,0:T(8,128)S(1)}, f32[2,64,512]{2,1,0:T(8,128)S(1)}, u32[]{:S(2)}, u32[]{:S(2)}) collective-permute-start(f32[2,64,512]{2,1,0:T(8,128)S(1)} %get-tuple-element.52), channel_id=1, source_target_pairs={{16,32},{48,64},{80,96},{112,128},{144,160},{176,192},{208,224},{3... | collective-permute-start | bytes 786440 | tf_op jit(solution)/shard_map/ppermute | solution.py:477
  6.5 17.9 %collective-permute-start = (f32[2,64,512]{2,1,0:T(8,128)S(1)}, f32[2,64,512]{2,1,0:T(8,128)S(1)}, u32[]{:S(2)}, u32[]{:S(2)}) collective-permute-start(f32[2,64,512]{2,1,0:T(8,128)S(1)} %get-tuple-element.53), channel_id=1, source_target_pairs={{0,16},{32,48},{64,80},{96,112},{128,144},{160,176},{192,208},{224... | collective-permute-start | bytes 786440 | tf_op jit(solution)/shard_map/ppermute | solution.py:477
  6.7 1.6 %copy-start = (f32[2,512,512]{2,1,0:T(8,128)S(1)}, f32[2,512,512]{2,1,0:T(8,128)}, u32[]{:S(2)}) copy-start(f32[2,512,512]{2,1,0:T(8,128)} %tile.5) | copy-start | bytes 6291460
  8.3 16.1 %copy-start.5 = (s32[2]{0:T(128)}, s32[2]{0:T(128)S(1)}, u32[]{:S(2)}) copy-start(s32[2]{0:T(128)S(1)} %pad_add_fusion.sides) | copy-start | bytes 28
  9.3 18.2 %collective-permute-start.2 = (f32[512,128]{1,0:T(8,128)S(1)}, f32[512,128]{1,0:T(8,128)S(1)}, u32[]{:S(2)}, u32[]{:S(2)}) collective-permute-start(f32[512,128]{1,0:T(8,128)S(1)} %get-tuple-element.31), channel_id=1, source_target_pairs={{0,1},{2,3},{4,5},{6,7},{8,9},{10,11},{12,13},{14,15},{1,0},{3,2},... | collective-permute-start | bytes 786440 | tf_op jit(solution)/shard_map/ppermute | solution.py:477
  10.3 17.2 %collective-permute-start.3 = (f32[512,128]{1,0:T(8,128)S(1)}, f32[512,128]{1,0:T(8,128)}, u32[]{:S(2)}, u32[]{:S(2)}) collective-permute-start(f32[512,128]{1,0:T(8,128)S(1)} %get-tuple-element.32), channel_id=1, source_target_pairs={{1,2},{3,4},{5,6},{7,8},{9,10},{11,12},{13,14},{2,1},{4,3},{6,5},{... | collective-permute-start | bytes 786440 | tf_op jit(solution)/shard_map/ppermute | solution.py:477
  24.4 6.5 %copy-start.1 = (f32[2,64,512]{2,1,0:T(8,128)}, f32[2,64,512]{2,1,0:T(8,128)S(1)}, u32[]{:S(2)}) copy-start(f32[2,64,512]{2,1,0:T(8,128)S(1)} %collective-permute-done.1.rows_b) | copy-start | bytes 786436
  24.5 6.5 %copy-start.2 = (f32[2,64,512]{2,1,0:T(8,128)}, f32[2,64,512]{2,1,0:T(8,128)S(1)}, u32[]{:S(2)}) copy-start(f32[2,64,512]{2,1,0:T(8,128)S(1)} %collective-permute-done.rows_a) | copy-start | bytes 786436
  25.3 2.2 %collective-permute-start.4 = (f32[128,128]{1,0:T(8,128)S(1)}, f32[128,128]{1,0:T(8,128)S(1)}, u32[]{:S(2)}, u32[]{:S(2)}) collective-permute-start(f32[128,128]{1,0:T(8,128)S(1)} %get-tuple-element.33), channel_id=1, source_target_pairs={{0,1},{2,3},{4,5},{6,7},{8,9},{10,11},{12,13},{14,15},{1,0},{3,2},... | collective-permute-start | bytes 196616 | tf_op jit(solution)/shard_map/ppermute | solution.py:477
  25.4 5.6 %collective-permute-start.5 = (f32[128,128]{1,0:T(8,128)S(1)}, f32[128,128]{1,0:T(8,128)S(1)}, u32[]{:S(2)}, u32[]{:S(2)}) collective-permute-start(f32[128,128]{1,0:T(8,128)S(1)} %get-tuple-element.34), channel_id=1, source_target_pairs={{1,2},{3,4},{5,6},{7,8},{9,10},{11,12},{13,14},{2,1},{4,3},{6,5},{... | collective-permute-start | bytes 196616 | tf_op jit(solution)/shard_map/ppermute | solution.py:477
  27.5 3.5 %copy-start.7 = (f32[512,128]{1,0:T(8,128)}, f32[512,128]{1,0:T(8,128)S(1)}, u32[]{:S(2)}) copy-start(f32[512,128]{1,0:T(8,128)S(1)} %collective-permute-done.2.cols_a) | copy-start | bytes 786436
  27.5 3.5 %copy-start.8 = (f32[128,128]{1,0:T(8,128)}, f32[128,128]{1,0:T(8,128)S(1)}, u32[]{:S(2)}) copy-start(f32[128,128]{1,0:T(8,128)S(1)} %collective-permute-done.4.corners_a) | copy-start | bytes 196612
  31.0 0.6 copy-start.9
  40.1 9.2 %collective-permute-start.8 = (f32[2,2,128,128]{3,2,1,0:T(8,128)}, f32[2,2,128,128]{3,2,1,0:T(8,128)S(1)}, u32[]{:S(2)}, u32[]{:S(2)}) collective-permute-start(f32[2,2,128,128]{3,2,1,0:T(8,128)} %get-tuple-element.41), channel_id=1, source_target_pairs={{0,1},{1,0},{2,3},{3,2},{4,5},{5,4},{6,7},{7,6},{8,9},{9,8},{10,11... | collective-permute-start | bytes 786440 | tf_op jit(solution)/shard_map/ppermute | solution.py:477
  51.1 22.4 %all-to-all-start = ((f32[16,32,128]{2,1,0:T(8,128)}), f32[16,32,128]{2,1,0:T(8,128)S(1)}, u32[]{:S(2)}, u32[]{:S(2)}) async-start(f32[16,32,128]{2,1,0:T(8,128)} %bitcast.4), calls=%async_computation | async-start | bytes 524288 | tf_op jit(solution)/shard_map/all_to_all | solution.py:487
  65.6 18.2 %copy-start.6 = (s32[2]{0:T(128)S(1)}, s32[2]{0:T(128)}, u32[]{:S(2)}) copy-start(s32[2]{0:T(128)} %copy-done.5) | copy-start | bytes 28
  70.5 12.3 %collective-permute-start.6 = (f32[640,128]{1,0:T(8,128)}, f32[640,128]{1,0:T(8,128)S(1)}, u32[]{:S(2)}, u32[]{:S(2)}) collective-permute-start(f32[640,128]{1,0:T(8,128)} %get-tuple-element.38), channel_id=1, source_target_pairs={{0,1},{2,3},{4,5},{6,7},{8,9},{10,11},{12,13},{14,15},{1,0},{3,2},... | collective-permute-start | bytes 983048 | tf_op jit(solution)/shard_map/ppermute | solution.py:477
  71.5 12.3 %collective-permute-start.7 = (f32[640,128]{1,0:T(8,128)}, f32[640,128]{1,0:T(8,128)S(1)}, u32[]{:S(2)}, u32[]{:S(2)}) collective-permute-start(f32[640,128]{1,0:T(8,128)} %get-tuple-element.39), channel_id=1, source_target_pairs={{1,2},{3,4},{5,6},{7,8},{9,10},{11,12},{13,14},{2,1},{4,3},{6,5},{... | collective-permute-start | bytes 983048 | tf_op jit(solution)/shard_map/ppermute | solution.py:477
  74.1 17.6 %all-to-all-start.1 = ((f32[8,32,128]{2,1,0:T(8,128)}), f32[8,32,128]{2,1,0:T(8,128)S(1)}, u32[]{:S(2)}, u32[]{:S(2)}) async-start(f32[8,32,128]{2,1,0:T(8,128)} %broadcast_in_dim.4), calls=%async_computation.1 | async-start | bytes 262144 | tf_op jit(solution)/shard_map/all_to_all | solution.py:492
  83.8 1.0 copy-start.3
  84.7 0.9 copy-start.4
  91.7 15.9 %collective-permute-start.9 = (f32[2,64,512]{2,1,0:T(8,128)S(1)}, f32[2,64,512]{2,1,0:T(8,128)S(1)}, u32[]{:S(2)}, u32[]{:S(2)}) collective-permute-start(f32[2,64,512]{2,1,0:T(8,128)S(1)} %get-tuple-element.47), channel_id=1, source_target_pairs={{0,16},{32,48},{64,80},{96,112},{128,144},{160,176},{192,208},{224... | collective-permute-start | bytes 786440 | tf_op jit(solution)/shard_map/ppermute | solution.py:477
  92.0 19.4 %collective-permute-start.10 = (f32[2,64,512]{2,1,0:T(8,128)S(1)}, f32[2,64,512]{2,1,0:T(8,128)S(1)}, u32[]{:S(2)}, u32[]{:S(2)}) collective-permute-start(f32[2,64,512]{2,1,0:T(8,128)S(1)} %get-tuple-element.48), channel_id=1, source_target_pairs={{16,32},{48,64},{80,96},{112,128},{144,160},{176,192},{208,224},{3... | collective-permute-start | bytes 786440 | tf_op jit(solution)/shard_map/ppermute | solution.py:477
  111.4 5.8 %collective-permute-start.11 = (f32[512,128]{1,0:T(8,128)S(1)}, f32[512,128]{1,0:T(8,128)S(1)}, u32[]{:S(2)}, u32[]{:S(2)}) collective-permute-start(f32[512,128]{1,0:T(8,128)S(1)} %bitcast.9), channel_id=1, source_target_pairs={{0,1},{1,0},{2,3},{3,2},{4,5},{5,4},{6,7},{7,6},{8,9},{9,8},{10,11... | collective-permute-start | bytes 786440 | tf_op jit(solution)/shard_map/ppermute | solution.py:477
